TPU v7x, 256 devices: a whole 4x4x8 slice. The times are simulated.
256 devices in a mesh: head: 16 (over z, core), pool: 16 (over y, x).
Axes of the slice: x: 4, y: 4, z: 8, core: 2. Of those that a mesh axis runs over, the one named last changes fastest.
Arguments:
- hidden_in: bfloat16 [64, 16384], P(None, 'pool'), may hold values from -6 to 6
- w_query: bfloat16 [16384, 16384], P('pool', 'head'), may hold values from -0.046875 to 0.046875
- w_key: bfloat16 [16384, 1024], P('pool', 'head'), may hold values from -0.046875 to 0.046875
- w_value: bfloat16 [16384, 1024], P('pool', 'head'), may hold values from -0.046875 to 0.046875
- w_out: bfloat16 [16384, 16384], P('head', 'pool'), may hold values from -0.046875 to 0.046875
- k_cache: bfloat16 [64, 6144, 1024], P('pool', 'head'), may hold values from -110 to 110
- v_cache: bfloat16 [64, 6144, 1024], P('pool', 'head'), may hold values from -6 to 6
- cache_len: int32 [64], replicated, may hold values from 1 to 6144, as said below
- slot_of: int32 [64], replicated, may hold values from 0 to 63, each once
Outputs:
- mixed: float32 [64, 16384], P('head', 'pool')
Inputs may be any that keep to these rules, and one draw needn't show every extreme that they name: `slot_of`: every slot holds exactly one request. `cache_len`: one request in every draw has exactly 6144 cached positions.
All inputs are finite; a program needn't handle non-finite values.
Results may differ from a plain program's by a relative error of at most 0.012.
The roundings to bfloat16 on the way count: a program that leaves them out, or rounds other values in their place, can miss the bound.
Values may be sent and summed in bfloat16 or wider, within the bound.
A program may use at most 64 MiB of HBM per device.

v0:
```python
import math

import jax
import jax.numpy as jnp
from jax import lax
from jax.sharding import PartitionSpec as P

QH = 128
KVH = 8
HD = 128


THETA = 500000.0
NEGATIVE = -1e30


def joined(value, axis, join):
    pieces = jax.tree.map(lambda part: lax.all_gather(part, axis), value)
    head = jax.tree.map(lambda part: part[0], pieces)
    tail = jax.tree.map(lambda part: part[1:], pieces)
    running, _ = lax.scan(lambda running, slab: (join(running, slab), None), head, tail)
    return running


def rotate(heads, positions):
    half_dim = heads.shape[-1] // 2
    offsets = jnp.arange(half_dim, dtype=jnp.float32)
    inverse = THETA ** (-2.0 * offsets / heads.shape[-1])
    angles = positions.astype(jnp.float32)[:, None] * inverse[None, :]
    cosine = jnp.cos(angles)[:, None, :]
    sine_part = jnp.sin(angles)[:, None, :]
    leading = heads[..., :half_dim]
    trailing = heads[..., half_dim:]
    return jnp.concatenate(
        [leading * cosine - trailing * sine_part, trailing * cosine + leading * sine_part], axis=-1
    )


def combine_partials(earlier, later):
    max_one, total_one, sums_one = earlier
    max_two, total_two, sums_two = later
    largest = jnp.maximum(max_one, max_two)
    factor_one = jnp.exp(max_one - largest)
    factor_two = jnp.exp(max_two - largest)
    return (
        largest,
        total_one * factor_one + total_two * factor_two,
        sums_one * factor_one[..., None] + sums_two * factor_two[..., None],
    )


def local(hidden_in, w_query, w_key, w_value, w_out, k_cache, v_cache, cache_len, slot_of):
    slots_here = k_cache.shape[0]
    span_here = k_cache.shape[1]
    head_count = lax.axis_size("head")
    head_rank = lax.axis_index("head")
    pool_rank = lax.axis_index("pool")
    requests = slot_of.shape[0]
    request_of_slot = jnp.zeros_like(slot_of).at[slot_of].set(jnp.arange(requests, dtype=jnp.int32))
    my_requests = lax.dynamic_slice_in_dim(request_of_slot, pool_rank * slots_here, slots_here)
    my_lengths = jnp.take(cache_len, my_requests)
    summed = lax.psum(
        jnp.concatenate(
            [
                jnp.dot(hidden_in, w_query, preferred_element_type=jnp.float32),
                jnp.dot(hidden_in, w_key, preferred_element_type=jnp.float32),
                jnp.dot(hidden_in, w_value, preferred_element_type=jnp.float32),
            ],
            axis=1,
        ),
        "pool",
    )
    projected = jnp.take(summed, my_requests, axis=0)
    gathered = lax.all_gather(projected[:, None, :], "head", axis=1, tiled=True)
    query_width = w_query.shape[1]
    key_width = w_key.shape[1]
    query = gathered[:, :, :query_width].reshape(slots_here, QH, HD)
    key_raw = gathered[:, :, query_width : query_width + key_width].reshape(slots_here, KVH, HD)
    value_new = (
        gathered[:, :, query_width + key_width :].reshape(slots_here, KVH, HD).astype(jnp.bfloat16)
    )
    query = rotate(query, my_lengths).astype(jnp.bfloat16)
    key_new = rotate(key_raw, my_lengths).astype(jnp.bfloat16)
    group_size = QH // KVH
    score_scale = 1.0 / math.sqrt(HD)
    query_groups = query.reshape(slots_here, KVH, group_size, HD)
    key_view = k_cache.reshape(slots_here, span_here, KVH, HD)
    value_view = v_cache.reshape(slots_here, span_here, KVH, HD)
    scores = (
        jnp.einsum("sgjd,stgd->sgjt", query_groups, key_view, preferred_element_type=jnp.float32)
        * score_scale
    )
    positions = head_rank * span_here + jnp.arange(span_here, dtype=jnp.int32)
    valid = (positions[None, :] < my_lengths[:, None])[:, None, None, :]
    own_scores = (
        jnp.einsum("sgjd,sgd->sgj", query_groups, key_new, preferred_element_type=jnp.float32)
        * score_scale
    )
    own_valid = head_rank == 0
    local_max = jnp.maximum(
        jnp.max(jnp.where(valid, scores, NEGATIVE), axis=-1),
        jnp.where(own_valid, own_scores, NEGATIVE),
    )
    weights = jnp.where(valid, jnp.exp(scores - local_max[..., None]), 0.0)
    own_weight = jnp.where(own_valid, jnp.exp(own_scores - local_max), 0.0)
    denominator = jnp.sum(weights, axis=-1) + own_weight
    own_rounded = lax.optimization_barrier(own_weight.astype(jnp.bfloat16)).astype(jnp.float32)
    numerator = jnp.einsum(
        "sgjt,stgd->sgjd",
        weights.astype(jnp.bfloat16),
        value_view,
        preferred_element_type=jnp.float32,
    )
    numerator = numerator + own_rounded[..., None] * value_new[:, :, None, :].astype(jnp.float32)
    local_max = local_max.reshape(slots_here, QH)
    denominator = denominator.reshape(slots_here, QH)
    numerator = numerator.reshape(slots_here, QH, HD)
    heads_here = QH // head_count
    largest, totals, partial_sums = joined(
        (local_max, denominator, numerator), "head", combine_partials
    )
    totals = lax.dynamic_slice_in_dim(totals, head_rank * heads_here, heads_here, 1)
    partial_sums = lax.dynamic_slice_in_dim(partial_sums, head_rank * heads_here, heads_here, 1)
    attention = (
        (partial_sums / totals[..., None]).astype(jnp.bfloat16).reshape(slots_here, heads_here * HD)
    )
    attention_rows = lax.all_gather(attention, "pool", axis=0, tiled=True)
    return lax.psum_scatter(
        jnp.dot(
            jnp.take(attention_rows, slot_of, axis=0), w_out, preferred_element_type=jnp.float32
        ),
        "head",
        scatter_dimension=0,
        tiled=True,
    )


def solution(mesh):
    in_specs = (
        P(None, "pool"),
        P("pool", "head"),
        P("pool", "head"),
        P("pool", "head"),
        P("head", "pool"),
        P("pool", "head", None),
        P("pool", "head", None),
        P(),
        P(),
    )
    out_specs = P("head", "pool")
    return jax.shard_map(local, mesh=mesh, in_specs=in_specs, out_specs=out_specs, check_vma=False)
```

profile of v0, /device:TPU:1, one launch (start us, length us, event | category | flops | bytes accessed | tf_op | source)
XLA Modules:
  0.0 341.9 jit_solution(13126949985053936776)
XLA Ops:
  6.5 2.3 fusion.38
  8.8 1.1 fusion.39
  10.0 1.1 fusion.40
  11.1 0.8 concatenate.16
  12.0 0.8 scatter_custom_fusion
  12.8 0.1 compare_and_fusion
  12.9 0.6 gather_fusion
  13.7 0.1 multiply_cosine_fusion
  13.8 94.5 %all-reduce.4.cloned.1.call-done = f32[64,1152]{1,0:T(8,128)} async-done(((f32[64,1152]{1,0:T(8,128)}), f32[64,1152]{1,0:T(8,128)}) %all-reduce.4.cloned.1.call-update) | async-done | bytes 294928 | tf_op jit(solution)/shard_map/psum | solution.py:62
  108.2 1.5 gather_fusion.1
  109.8 20.0 %all_gather.15 = f32[4,16,1152]{2,0,1:T(4,128)S(1)} all-gather(f32[4,1,1152]{2,0,1:T(4,128)S(1)} %bitcast_select_fusion), channel_id=1, replica_groups=mesh['head'=16,'pool'=16] {'head'}, dimensions={1}, use_global_device_ids=true | all-gather | bytes 313344 | tf_op jit(solution)/shard_map/all_gather | solution.py:74
  130.0 0.9 copy.22
  130.9 1.0 reshape.157
  131.9 0.1 subtract_convert_fusion
  132.1 0.1 maximum_bitcast_fusion
  132.2 0.2 fusion.25
  132.4 1.3 select_reduce_fusion
  133.8 0.9 copy-done.2
  134.7 0.3 fusion.16
  135.1 3.6 %fusion.12 = f32[4,8,16,128]{3,2,1,0:T(8,128)} fusion(f32[4,8,16,384]{3,2,1,0:T(8,128)} %copy-done.2, f32[4,8,16]{2,1,0:T(8,128)S(1)} %select_maximum_fusion, pred[4,384]{1,0:T(4,128)(4,1)S(1)} %broadcast_compare_fusion, f32[4,8,128]{2,1,0:T(8,128)S(1)} %reshape.162, f32[4,8,16]{2,1,0:T(8,128)S(1)} %convert_element_type.41, bf16[4,384,1024]{2,1,0:T(8,128)(2,1)} %param.17), kind=kOutput, calls=%fused_computation.19 | convolution fusion | flops 51052544 | bytes 4216320 | tf_op jit(solution)/shard_map/sgjt,stgd->sgjd/dot_general | solution.py:108
  138.9 15.1 %all_gather.17 = f32[16,4,128]{2,1,0:T(4,128)S(1)} all-gather(f32[1,4,128]{2,1,0:T(4,128)S(1)} %all_gather_reshape.10), channel_id=1, replica_groups=mesh['head'=16,'pool'=16] {'head'}, dimensions={0}, use_global_device_ids=true | all-gather | bytes 34816 | tf_op jit(solution)/shard_map/all_gather | solution.py:18
  154.0 15.3 %all_gather.16 = f32[16,4,128]{2,1,0:T(4,128)S(1)} all-gather(f32[1,4,128]{2,1,0:T(4,128)S(1)} %all_gather_reshape.9), channel_id=1, replica_groups=mesh['head'=16,'pool'=16] {'head'}, dimensions={0}, use_global_device_ids=true | all-gather | bytes 34816 | tf_op jit(solution)/shard_map/all_gather | solution.py:18
  169.3 8.1 %all-gather.3.cloned.1.call-done = f32[16,4,128,128]{3,2,1,0:T(8,128)} async-done(((f32[1,4,128,128]{3,2,1,0:T(8,128)}), f32[16,4,128,128]{3,2,1,0:T(8,128)}) %all-gather.3.cloned.1.call-update) | async-done | bytes 4194320 | tf_op jit(solution)/shard_map/all_gather | solution.py:18
  177.4 4.5 %slice.71 = f32[15,4,128,128]{3,2,1,0:T(8,128)} slice(f32[16,4,128,128]{3,2,1,0:T(8,128)} %all-gather.3.cloned.1.call-done), slice={[1:16], [0:4], [0:128], [0:128]} | slice | bytes 7864320 | tf_op jit(solution)/shard_map/slice | solution.py:20
  181.9 1.0 slice_bitcast_fusion
  182.8 18.8 %while.14 = (s32[]{:T(128)}, f32[4,128]{1,0:T(4,128)S(1)}, f32[4,128]{1,0:T(4,128)S(1)}, f32[4,128,128]{2,1,0:T(8,128)S(1)}, f32[15,4,128]{2,1,0:T(4,128)S(1)}, ...) while((s32[]{:T(128)}, f32[4,128]{1,0:T(4,128)S(1)}, f32[4,128]{1,0:T(4,128)S(1)}, ...), condition=%wide.region_5.6_spmd, body=%wide.region_4.5_spmd.sunk | while | flops 199682 | bytes 807005 | solution.py:21
  182.9 1.2 fusion.53
  184.1 1.2 fusion.53
  185.4 1.2 fusion.53
  186.6 1.2 fusion.53
  187.9 1.2 fusion.53
  189.2 1.2 fusion.53
  190.4 1.2 fusion.53
  191.7 1.2 fusion.53
  192.9 1.2 fusion.53
  194.2 1.2 fusion.53
  195.4 1.2 fusion.53
  196.7 1.2 fusion.53
  197.9 1.2 fusion.53
  199.2 1.2 fusion.53
  200.4 1.2 fusion.53
  201.7 0.1 divide_convert_fusion
  201.8 18.5 %all-gather = bf16[16,4,1024]{2,1,0:T(4,128)(2,1)S(1)} all-gather(bf16[1,4,1024]{2,1,0:T(4,128)(2,1)S(1)} %reshape.199), channel_id=1, replica_groups=mesh['head'=16,'pool'=16] {'pool'}, dimensions={0}, use_global_device_ids=true | all-gather | bytes 139264 | tf_op jit(solution)/shard_map/all_gather | solution.py:127
  220.4 0.7 gather_fusion.2
  221.1 2.8 fusion.21
  223.9 0.6 dynamic-slice
  225.2 108.8 %all-reduce.6.cloned.1.call-done = f32[64,1024]{1,0:T(8,128)} async-done(((f32[64,1024]{1,0:T(8,128)}), f32[64,1024]{1,0:T(8,128)}) %all-reduce.6.cloned.1.call-update) | async-done | bytes 262160
  334.0 1.4 constant_dynamic-slice_fusion
  (60 shorter events, 1.4 us)
Async XLA Ops:
  6.5 125.9 %copy-start = (bf16[4,384,1024]{2,1,0:T(8,128)(2,1)S(1)}, bf16[4,384,1024]{2,1,0:T(8,128)(2,1)}, u32[]{:S(2)}) copy-start(bf16[4,384,1024]{2,1,0:T(8,128)(2,1)} %param.16) | copy-start | bytes 9437188
  6.5 5.5 %copy-start.3 = (s32[64]{0:T(128)S(1)}, s32[64]{0:T(128)}, u32[]{:S(2)}) copy-start(s32[64]{0:T(128)} %param.19) | copy-start | bytes 772
  6.5 6.4 %copy-start.1 = (s32[64]{0:T(128)S(1)}, s32[64]{0:T(128)}, u32[]{:S(2)}) copy-start(s32[64]{0:T(128)} %param.18) | copy-start | bytes 772
  6.5 101.7 %all-reduce.4.cloned.1.call-start = ((), (), s32[]{:S(2)}) async-start(), calls=%async_computation | async-start | bytes 589824 | tf_op jit(solution)/shard_map/psum | solution.py:62
  11.9 165.5 %all-gather.3.cloned.1.call-start = ((), (), s32[]{:S(2)}) async-start(), calls=%async_computation.1 | async-start | bytes 4456448 | tf_op jit(solution)/shard_map/all_gather | solution.py:18
  133.8 0.9 copy-start.2
  138.7 195.3 %all-reduce.6.cloned.1.call-start = ((), (), s32[]{:S(2)}) async-start(), calls=%async_computation.2 | async-start | bytes 524288
  201.7 22.3 %copy-start.4 = (u32[256]{0:T(256)S(1)}, u32[256]{0:T(256)}, u32[]{:S(2)}) copy-start(u32[256]{0:T(256)} %constant.91) | copy-start | bytes 3076
Sparse Core Ops, SparseCore 0:
  12.1 96.1 all-reduce.3
  138.8 38.5 all-gather.2
  224.0 109.8 all-reduce.5
where the time goes:
time: 343 us; the launch traced here: 342 us
  waiting for transfers between devices  211 us (62%)
  blocking collectives  68.8 us (20%)
  other arithmetic  19.6 us (6%)
  local copies, waits for them, and re-layouts  15.1 us (4%)
  between operations  14 us (4%)
  matrix products  12.6 us (4%)
    unnamed x4, waiting for transfers between devices  109 us
    psum x1, waiting for transfers between devices, local(): lax.psum(jnp.concatenate([jnp.dot(hidden_in, w_query, preferred_element_t...  94.5 us
    all_gather x2, blocking collectives, joined(): pieces = jax.tree.map(lambda part: lax.all_gather(part, axis), value)  30.4 us
    all_gather x1, blocking collectives, local(): gathered = lax.all_gather(projected[:, None, :], 'head', axis=1, tiled=True)  20 us
    all_gather x1, blocking collectives, local(): attention_rows = lax.all_gather(attention, 'pool', axis=0, tiled=True)  18.5 us
    add x15, other arithmetic, combine_partials(): sums_one * factor_one[..., None] + sums_two * factor_two[..., None]  18.1 us
    all_gather x1, waiting for transfers between devices, joined(): pieces = jax.tree.map(lambda part: lax.all_gather(part, axis), value)  8.08 us
  transfers between devices with their start and end apart: 3, of which 3 were waited for; matrix products, arithmetic and copies ran while one was open for 1% of the time, Pallas kernels for 0%

commit v1 on v0

v1 whole, which is shorter than its diff:
```python
import functools
import math

import jax
import jax.numpy as jnp
import numpy as np
from jax import lax
from jax.experimental import pallas as pl
from jax.experimental.pallas import tpu as pltpu
from jax.sharding import PartitionSpec as P

QH = 128
KVH = 8
HD = 128
THETA = 500000.0
NEGATIVE = -1e30
MESH = pl.DeviceIdType.MESH
F32 = jnp.float32
BF16 = jnp.bfloat16

POOL_OFFSETS = sorted(
    [(dy, dx) for dy in range(4) for dx in range(4) if (dy, dx) != (0, 0)],
    key=lambda o: -(min(o[0], 4 - o[0]) + min(o[1], 4 - o[1])),
)
HEAD_OFFSETS = sorted(
    [(dz, dc) for dz in range(8) for dc in range(2) if (dz, dc) != (0, 0)],
    key=lambda o: -(min(o[0], 8 - o[0]) + 0.5 * o[1]),
)


def pair_rows(x):
    row = lax.broadcasted_iota(jnp.int32, (8, 8, 128), 1)
    left = x[:, :128].reshape(8, 8, 128)
    right = x[:, 128:].reshape(8, 8, 128)
    even = jnp.where(row < 4, left, pltpu.roll(right, 4, 1))
    odd = jnp.where(row < 4, pltpu.roll(left, 4, 1), right)
    return jnp.stack([even, odd], axis=1).reshape(16, 8, 128)


def kernel(
    hid_hbm, wq_hbm, wk_hbm, wv_hbm, wo_hbm, k_hbm, v_hbm, len_ref, slot_ref, inv_ref, out_ref,
    hid, wq, wk, wv, wo, kc, vc,
    s1, r1, qf, s2, r2, skv, rkv, s4, r4, st4, rt4, s5, r5, s6, r6, sel,
    load_sem, send_sem, recv_sem, kv_sem,
):
    head = lax.axis_index("head")
    pool = lax.axis_index("pool")
    z, core = head // 2, head % 2
    py, px = pool // 4, pool % 4

    def pool_peer(offset):
        return lax.rem(py + offset[0], 4) * 4 + lax.rem(px + offset[1], 4)

    def head_peer(offset):
        return lax.rem(z + offset[0], 8) * 2 + lax.rem(core + offset[1], 2)

    def pool_send(src, dst, phase, offset):
        pltpu.make_async_remote_copy(
            src, dst, send_sem.at[phase], recv_sem.at[phase],
            device_id=(head, pool_peer(offset)), device_id_type=MESH,
        ).start()

    def head_send(src, dst, phase, offset):
        pltpu.make_async_remote_copy(
            src, dst, send_sem.at[phase], recv_sem.at[phase],
            device_id=(head_peer(offset), pool), device_id_type=MESH,
        ).start()

    def wait_all(buf, sem):
        pltpu.make_async_copy(buf.at[pl.ds(0, 15)], buf.at[pl.ds(0, 15)], sem).wait()

    loads = [
        pltpu.make_async_copy(hid_hbm, hid, load_sem.at[0]),
        pltpu.make_async_copy(wk_hbm, wk, load_sem.at[1]),
        pltpu.make_async_copy(wv_hbm, wv, load_sem.at[2]),
    ]
    for c in range(4):
        cols = pl.ds(256 * c, 256)
        loads.append(pltpu.make_async_copy(wq_hbm.at[:, cols], wq.at[:, cols], load_sem.at[3 + c]))
    loads.append(pltpu.make_async_copy(k_hbm, kc, load_sem.at[7]))
    loads.append(pltpu.make_async_copy(v_hbm, vc, load_sem.at[8]))
    loads.append(pltpu.make_async_copy(wo_hbm, wo, load_sem.at[9]))
    for copy in loads:
        copy.start()

    barrier = pltpu.get_barrier_semaphore()
    for offset in POOL_OFFSETS:
        pl.semaphore_signal(barrier, inc=1, device_id=(head, pool_peer(offset)), device_id_type=MESH)
    for offset in HEAD_OFFSETS:
        pl.semaphore_signal(barrier, inc=1, device_id=(head_peer(offset), pool), device_id_type=MESH)

    slot_row = slot_ref[...]
    len_row = len_ref[...].astype(F32)
    to_slot = (lax.broadcasted_iota(jnp.int32, (64, 64), 0) == slot_row).astype(BF16)
    mine = pool * 4 + lax.broadcasted_iota(jnp.int32, (8, 64), 0) % 4
    lengths = jnp.sum(jnp.where(mine == slot_row, len_row, 0.0), axis=1, keepdims=True)
    angle = lengths * inv_ref[...]
    lane = lax.broadcasted_iota(jnp.int32, (8, 128), 1)
    cosine = jnp.cos(angle)
    sine = jnp.where(lane < 64, -jnp.sin(angle), jnp.sin(angle))

    def rotate(x):
        return x * cosine + pltpu.roll(x, 64, 1) * sine

    loads[0].wait()
    hidden = jnp.dot(to_slot, hid[...], preferred_element_type=F32).astype(BF16)

    loads[1].wait()
    loads[2].wait()
    zeros = jnp.zeros((64, 64), F32)
    across = (((1,), (1,)), ((), ()))
    key_part = lax.dot_general(hidden, wk[...], across, preferred_element_type=F32)
    value_part = lax.dot_general(hidden, wv[...], across, preferred_element_type=F32)
    s1[:, 32:40, :] = pair_rows(jnp.concatenate([key_part, zeros, value_part, zeros], axis=1))
    for c in range(4):
        loads[3 + c].wait()
        s1[:, 8 * c : 8 * c + 8, :] = pair_rows(
            jnp.dot(hidden, wq[:, 256 * c : 256 * c + 256], preferred_element_type=F32)
        )
    pl.semaphore_wait(barrier, 30)
    for i, offset in enumerate(POOL_OFFSETS):
        pool_send(s1.at[pool_peer(offset)], r1.at[i], 0, offset)

    eye = lax.broadcasted_iota(jnp.int32, (64, 64), 0) == lax.broadcasted_iota(jnp.int32, (64, 64), 1)
    slot_col = jnp.sum(jnp.where(eye, slot_row.astype(F32), 0.0), axis=1, keepdims=True).astype(jnp.int32)
    column = lax.broadcasted_iota(jnp.int32, (64, 512), 1)
    for j in range(8):
        sel[64 * j : 64 * j + 64, :] = (slot_col * 8 + j == column).astype(BF16)

    wait_all(r1, recv_sem.at[0])
    total = s1[pool]
    for i in range(15):
        total = total + r1[i]

    skv[...] = total[32:40]
    kv_copy = pltpu.make_async_remote_copy(
        skv, rkv, kv_sem.at[0], kv_sem.at[1], device_id=(z * 2 + 1 - core, pool), device_id_type=MESH
    )
    for c in range(4):
        qf[8 * c : 8 * c + 8, :] = rotate(total[8 * c : 8 * c + 8])
    query = jnp.concatenate([qf[pl.ds(s, 8, stride=4), :] for s in range(4)], axis=0).astype(BF16)
    s2[...] = query
    r2[head] = query
    for offset in HEAD_OFFSETS:
        head_send(s2, r2.at[head], 1, offset)
    kv_copy.start()
    own_query = query.astype(F32).reshape(4, 8, 128)
    kv_copy.wait()
    here, there = skv[...], rkv[...]
    even = jnp.where(lane < 64, here, pltpu.roll(there, 64, 1))
    odd = jnp.where(lane < 64, there, pltpu.roll(here, 64, 1))
    key_value = jnp.where(core == 0, even, odd)
    key_new = rotate(key_value).astype(BF16).astype(F32)
    value_new = key_value.astype(BF16).astype(F32)
    scale = 1.0 / math.sqrt(HD)
    own = jnp.full((8, 128), NEGATIVE, F32)
    for s in range(4):
        score = jnp.sum(own_query[s] * key_new[s : s + 1, :], axis=1, keepdims=True) * scale
        own = jnp.where(lane == s, score, own)

    wait_all(r2, recv_sem.at[1])
    loads[7].wait()
    loads[8].wait()
    queries = r2[...].astype(F32).reshape(16, 4, 8, 128)
    place = (head * 384 + lax.broadcasted_iota(jnp.int32, (1, 384), 1)).astype(F32)
    wide_lane = lax.broadcasted_iota(jnp.int32, (128, 128), 1)
    stats = jnp.zeros((128, 128), F32)
    sums = []
    for s in range(4):
        q = queries[:, s].reshape(128, 128).astype(BF16)
        scores = jnp.concatenate(
            [
                lax.dot_general(
                    q[16 * g : 16 * g + 16], kc[s, :, 128 * g : 128 * g + 128],
                    across, preferred_element_type=F32,
                )
                for g in range(KVH)
            ],
            axis=0,
        ) * scale
        valid = place < lengths[s : s + 1, :]
        top = jnp.max(jnp.where(valid, scores, NEGATIVE), axis=1, keepdims=True)
        weights = jnp.where(valid, jnp.exp(scores - top), 0.0)
        bottom = jnp.sum(weights, axis=1, keepdims=True)
        weights = weights.astype(BF16)
        sums.append(
            jnp.concatenate(
                [
                    jnp.dot(
                        weights[16 * g : 16 * g + 16], vc[s, :, 128 * g : 128 * g + 128],
                        preferred_element_type=F32,
                    )
                    for g in range(KVH)
                ],
                axis=0,
            ).reshape(16, 8, 128)
        )
        stats = jnp.where(wide_lane == s, top, jnp.where(wide_lane == 4 + s, bottom, stats))

    st4[...] = stats.reshape(16, 8, 128)
    s4[...] = jnp.concatenate(sums, axis=1).astype(BF16)
    for i, offset in enumerate(HEAD_OFFSETS):
        head_send(st4.at[head_peer(offset)], rt4.at[i], 2, offset)
        head_send(s4.at[head_peer(offset)], r4.at[i], 3, offset)
    wait_all(rt4, recv_sem.at[2])
    parts = [rt4[i] for i in range(15)] + [st4[head]]
    largest = own
    for part in parts:
        largest = jnp.maximum(largest, part)
    own_weight = jnp.exp(own - largest)
    denominator = own_weight
    factors = []
    for part in parts:
        factor = jnp.exp(part - largest)
        denominator = denominator + factor * pltpu.roll(part, 124, 1)
        factors.append(factor)
    own_weight = own_weight.astype(BF16).astype(F32)
    numerator = [own_weight[:, s : s + 1] * value_new[4 + s : 5 + s, :] for s in range(4)]
    wait_all(r4, recv_sem.at[3])
    for i in range(16):
        part = (r4[i] if i < 15 else s4[head]).astype(F32)
        for s in range(4):
            numerator[s] = numerator[s] + factors[i][:, s : s + 1] * part[8 * s : 8 * s + 8]
    attention = jnp.concatenate(
        [numerator[s] / denominator[:, s : s + 1] for s in range(4)], axis=0
    ).astype(BF16)

    s5[...] = attention
    r5[pool] = attention
    for offset in POOL_OFFSETS:
        pool_send(s5, r5.at[pool], 4, offset)
    loads[9].wait()
    wait_all(r5, recv_sem.at[4])
    rows = jnp.dot(sel[...], r5[...].reshape(512, 128), preferred_element_type=F32).astype(BF16)
    rows = jnp.concatenate([rows[64 * j : 64 * j + 64] for j in range(8)], axis=1)

    for c in range(2):
        pairs = [
            pair_rows(jnp.dot(rows, wo[:, 256 * i : 256 * i + 256], preferred_element_type=F32))
            for i in (2 * c, 2 * c + 1)
        ]
        s6[:, 16 * c : 16 * c + 16, :] = jnp.concatenate(pairs, axis=1).astype(BF16)
    for i, offset in enumerate(HEAD_OFFSETS):
        head_send(s6.at[head_peer(offset)], r6.at[i], 5, offset)
    wait_all(r6, recv_sem.at[5])
    mixed = s6[head].astype(F32)
    for i in range(15):
        mixed = mixed + r6[i].astype(F32)
    for c in range(4):
        out_ref[:, 256 * c : 256 * c + 128] = mixed[8 * c : 8 * c + 4]
        out_ref[:, 256 * c + 128 : 256 * c + 256] = mixed[8 * c + 4 : 8 * c + 8]

    wait_all(r1, send_sem.at[0])
    wait_all(r2, send_sem.at[1])
    wait_all(rt4, send_sem.at[2])
    wait_all(r4, send_sem.at[3])
    wait_all(r5, send_sem.at[4])
    wait_all(r6, send_sem.at[5])


def local(hidden_in, w_query, w_key, w_value, w_out, k_cache, v_cache, cache_len, slot_of):
    half = np.arange(128) % 64
    inverse = np.broadcast_to((THETA ** (-2.0 * half / HD)).astype(np.float32)[None], (8, 128))
    hbm = pl.BlockSpec(memory_space=pl.ANY)
    vmem = pl.BlockSpec(memory_space=pltpu.VMEM)
    return pl.pallas_call(
        kernel,
        out_shape=jax.ShapeDtypeStruct((4, 1024), F32),
        in_specs=[hbm] * 7 + [vmem] * 3,
        out_specs=vmem,
        scratch_shapes=[
            pltpu.VMEM((64, 1024), BF16),
            pltpu.VMEM((1024, 1024), BF16),
            pltpu.VMEM((64, 1024), BF16),
            pltpu.VMEM((64, 1024), BF16),
            pltpu.VMEM((1024, 1024), BF16),
            pltpu.VMEM((4, 384, 1024), BF16),
            pltpu.VMEM((4, 384, 1024), BF16),
            pltpu.VMEM((16, 40, 128), F32),
            pltpu.VMEM((15, 40, 128), F32),
            pltpu.VMEM((32, 128), F32),
            pltpu.VMEM((32, 128), BF16),
            pltpu.VMEM((16, 32, 128), BF16),
            pltpu.VMEM((8, 128), F32),
            pltpu.VMEM((8, 128), F32),
            pltpu.VMEM((16, 32, 128), BF16),
            pltpu.VMEM((15, 32, 128), BF16),
            pltpu.VMEM((16, 8, 128), F32),
            pltpu.VMEM((15, 8, 128), F32),
            pltpu.VMEM((32, 128), BF16),
            pltpu.VMEM((16, 32, 128), BF16),
            pltpu.VMEM((16, 32, 128), BF16),
            pltpu.VMEM((15, 32, 128), BF16),
            pltpu.VMEM((512, 512), BF16),
            pltpu.SemaphoreType.DMA((10,)),
            pltpu.SemaphoreType.DMA((6,)),
            pltpu.SemaphoreType.DMA((6,)),
            pltpu.SemaphoreType.DMA((2,)),
        ],
        compiler_params=pltpu.CompilerParams(
            collective_id=0, has_side_effects=True, vmem_limit_bytes=48 * 1024 * 1024
        ),
    )(
        hidden_in, w_query, w_key.T, w_value.T, w_out, k_cache, v_cache,
        cache_len.reshape(1, 64), slot_of.reshape(1, 64), jnp.asarray(inverse),
    )


def solution(mesh):
    in_specs = (
        P(None, "pool"),
        P("pool", "head"),
        P("pool", "head"),
        P("pool", "head"),
        P("head", "pool"),
        P("pool", "head", None),
        P("pool", "head", None),
        P(),
        P(),
    )
    out_specs = P("head", "pool")
    return jax.shard_map(local, mesh=mesh, in_specs=in_specs, out_specs=out_specs, check_vma=False)
```

time: 343 us -> 50.6 us (0.15)
  waiting for transfers between devices: 211 us -> 0 us
  blocking collectives: 68.8 us -> 0 us
  Pallas kernels: 0 us -> 41.9 us
  other arithmetic: 19.6 us -> 0 us
  between operations: 14 us -> 0.02 us
  matrix products: 12.6 us -> 0 us
  local copies, waits for them, and re-layouts: 15.1 us -> 8.47 us
    unnamed x4 -> x0, waiting for transfers between devices: 109 us -> none
    psum x1 -> x0, waiting for transfers between devices: 94.5 us -> none  [local(): lax.psum(jnp.concatenate([jnp.dot(hidden_in, w_query, preferred_element_t...]
    all_gather x4 -> x0, blocking collectives: 68.8 us -> none  [the longest x2 30.4 us: joined(): pieces = jax.tree.map(lambda part: lax.all_gather(part, axis), value)]
    pallas_call x0 -> x1, Pallas kernels: none -> 41.9 us  [local(): pl.pallas_call(kernel, out_shape=jax.ShapeDtypeStruct((4, 1024), F32), in...]
    add x31 -> x0, other arithmetic: 18.5 us -> none  [the longest x15 18.1 us: combine_partials(): sums_one * factor_one[..., None] + sums_two * factor_two[..., None]]
    dot_general x7 -> x0, matrix products: 12.6 us -> none  [the longest x1 3.61 us: local(): jnp.einsum('sgjt,stgd->sgjd', weights.astype(jnp.bfloat16), value_view, p...]
    all_gather x1 -> x0, waiting for transfers between devices: 8.08 us -> none  [joined(): pieces = jax.tree.map(lambda part: lax.all_gather(part, axis), value)]
    slice x8 -> x0, local copies, waits for them, and re-layouts: 5.42 us -> none  [the longest x3 4.46 us: joined(): tail = jax.tree.map(lambda part: part[1:], pieces)]
  transfers between devices with their start and end apart: 3 -> 0, of which waited for: 3 -> 0; matrix products, arithmetic and copies ran while one was open for 1% -> 0% of each run, Pallas kernels for 0% -> 0%
where the time goes in v1:
time: 50.6 us; the launch traced here: 50.4 us
  Pallas kernels  41.9 us (83%)
  local copies, waits for them, and re-layouts  8.47 us (17%)
    pallas_call x1, Pallas kernels, local(): pl.pallas_call(kernel, out_shape=jax.ShapeDtypeStruct((4, 1024), F32), in...  41.9 us
    unnamed x15, local copies, waits for them, and re-layouts  7.81 us

profile of v1, /device:TPU:1, one launch (start us, length us, event | category | flops | bytes accessed | tf_op | source)
XLA Modules:
  0.0 50.4 jit_solution(625216980432793753)
XLA Ops:
  0.0 0.7 %jit_solution_.3.inv_ref = f32[8,128]{1,0:T(8,128)S(1)} broadcast(f32[128]{0:T(128)} %constant.2.clone), dimensions={1} | broadcast | bytes 4608 | tf_op jit(solution)
  0.7 0.0 copy-start
  0.7 1.6 %copy-done = bf16[1024,1024]{1,0:T(8,128)(2,1)S(1)} copy-done((bf16[1024,1024]{1,0:T(8,128)(2,1)S(1)}, bf16[1024,1024]{1,0:T(8,128)(2,1)}, u32[]{:S(2)}) %copy-start) | copy-done | bytes 2097176
  2.2 0.0 copy-start.1
  2.3 1.6 %copy-done.1 = bf16[1024,1024]{1,0:T(8,128)(2,1)S(1)} copy-done((bf16[1024,1024]{1,0:T(8,128)(2,1)S(1)}, bf16[1024,1024]{1,0:T(8,128)(2,1)}, u32[]{:S(2)}) %copy-start.1) | copy-done | bytes 2097176
  3.8 0.0 copy-start.2
  3.8 0.9 %copy-done.2 = bf16[64,1024]{1,0:T(8,128)(2,1)S(1)} copy-done((bf16[64,1024]{1,0:T(8,128)(2,1)S(1)}, bf16[64,1024]{1,0:T(8,128)(2,1)}, u32[]{:S(2)}) %copy-start.2) | copy-done | bytes 131096
  4.7 0.0 copy-start.3
  4.7 0.9 %copy-done.3 = bf16[1024,64]{0,1:T(8,128)(2,1)S(1)} copy-done((bf16[1024,64]{0,1:T(8,128)(2,1)S(1)}, bf16[1024,64]{0,1:T(8,128)(2,1)}, u32[]{:S(2)}) %copy-start.3) | copy-done | bytes 131096
  5.6 0.0 copy-start.4
  5.7 0.9 %copy-done.4 = bf16[1024,64]{0,1:T(8,128)(2,1)S(1)} copy-done((bf16[1024,64]{0,1:T(8,128)(2,1)S(1)}, bf16[1024,64]{0,1:T(8,128)(2,1)}, u32[]{:S(2)}) %copy-start.4) | copy-done | bytes 131096
  6.6 0.0 copy-start.5
  6.6 0.7 %copy-done.5 = s32[64]{0:T(128)S(1)} copy-done((s32[64]{0:T(128)S(1)}, s32[64]{0:T(128)}, u32[]{:S(2)}) %copy-start.5) | copy-done | bytes 280
  7.2 0.0 copy-start.6
  7.2 0.7 %copy-done.6 = s32[64]{0:T(128)S(1)} copy-done((s32[64]{0:T(128)S(1)}, s32[64]{0:T(128)}, u32[]{:S(2)}) %copy-start.6) | copy-done | bytes 280
  7.9 41.9 %shard_map.100 = f32[4,1024]{1,0:T(4,128)S(1)} custom-call(bf16[64,1024]{1,0:T(8,128)(2,1)S(1)} %copy-done.2, bf16[1024,1024]{1,0:T(8,128)(2,1)S(1)} %copy-done, bf16[64,1024]{1,0:T(8,128)(2,1)S(1)} %bitcast.4, bf16[64,1024]{1,0:T(8,128)(2,1)S(1)} %bitcast.5, bf16[1024,1024]{1,0:T(8,128)(2,1)S(1)} %copy-done.1, bf16[4,384,1024]{2,1,0:T(8,128)(2,1)} %k_hbm.1, ...), custom_call_target="tpu_custom_call" | custom-call | tf_op jit(solution)/shard_map/pallas_call | solution.py:266
  49.8 0.6 %copy.12 = f32[4,1024]{1,0:T(4,128)} copy(f32[4,1024]{1,0:T(4,128)S(1)} %shard_map.100) | data formatting | bytes 32768
Async XLA Ops:
  0.7 1.6 %copy-start = (bf16[1024,1024]{1,0:T(8,128)(2,1)S(1)}, bf16[1024,1024]{1,0:T(8,128)(2,1)}, u32[]{:S(2)}) copy-start(bf16[1024,1024]{1,0:T(8,128)(2,1)} %wq_hbm.1) | copy-start | bytes 6291460
  2.2 1.6 %copy-start.1 = (bf16[1024,1024]{1,0:T(8,128)(2,1)S(1)}, bf16[1024,1024]{1,0:T(8,128)(2,1)}, u32[]{:S(2)}) copy-start(bf16[1024,1024]{1,0:T(8,128)(2,1)} %wo_hbm.1) | copy-start | bytes 6291460
  3.8 0.9 %copy-start.2 = (bf16[64,1024]{1,0:T(8,128)(2,1)S(1)}, bf16[64,1024]{1,0:T(8,128)(2,1)}, u32[]{:S(2)}) copy-start(bf16[64,1024]{1,0:T(8,128)(2,1)} %hid_hbm.1) | copy-start | bytes 393220
  4.7 0.9 %copy-start.3 = (bf16[1024,64]{0,1:T(8,128)(2,1)S(1)}, bf16[1024,64]{0,1:T(8,128)(2,1)}, u32[]{:S(2)}) copy-start(bf16[1024,64]{0,1:T(8,128)(2,1)} %param.12) | copy-start | bytes 393220
  5.6 0.9 %copy-start.4 = (bf16[1024,64]{0,1:T(8,128)(2,1)S(1)}, bf16[1024,64]{0,1:T(8,128)(2,1)}, u32[]{:S(2)}) copy-start(bf16[1024,64]{0,1:T(8,128)(2,1)} %param.13) | copy-start | bytes 393220
  6.6 0.7 %copy-start.5 = (s32[64]{0:T(128)S(1)}, s32[64]{0:T(128)}, u32[]{:S(2)}) copy-start(s32[64]{0:T(128)} %param.17) | copy-start | bytes 772
  7.2 0.7 %copy-start.6 = (s32[64]{0:T(128)S(1)}, s32[64]{0:T(128)}, u32[]{:S(2)}) copy-start(s32[64]{0:T(128)} %param.18) | copy-start | bytes 772

commit v2 on v1

--- a/solution.py
+++ b/solution.py
@@ -1,9 +1,7 @@
-import functools
 import math
 
 import jax
 import jax.numpy as jnp
-import numpy as np
 from jax import lax
 from jax.experimental import pallas as pl
 from jax.experimental.pallas import tpu as pltpu
@@ -38,8 +36,8 @@
 
 
 def kernel(
-    hid_hbm, wq_hbm, wk_hbm, wv_hbm, wo_hbm, k_hbm, v_hbm, len_ref, slot_ref, inv_ref, out_ref,
-    hid, wq, wk, wv, wo, kc, vc,
+    hid_hbm, wq_hbm, wk_hbm, wv_hbm, wo_hbm, k_hbm, v_hbm, len_hbm, slot_hbm, out_ref,
+    len_ref, slot_ref, hid, wq, wk, wv, wo, kc, vc,
     s1, r1, qf, s2, r2, skv, rkv, s4, r4, st4, rt4, s5, r5, s6, r6, sel,
     load_sem, send_sem, recv_sem, kv_sem,
 ):
@@ -80,7 +78,11 @@
     loads.append(pltpu.make_async_copy(k_hbm, kc, load_sem.at[7]))
     loads.append(pltpu.make_async_copy(v_hbm, vc, load_sem.at[8]))
     loads.append(pltpu.make_async_copy(wo_hbm, wo, load_sem.at[9]))
-    for copy in loads:
+    small = [
+        pltpu.make_async_copy(len_hbm, len_ref, load_sem.at[10]),
+        pltpu.make_async_copy(slot_hbm, slot_ref, load_sem.at[11]),
+    ]
+    for copy in small + loads:
         copy.start()
 
     barrier = pltpu.get_barrier_semaphore()
@@ -89,13 +91,20 @@
     for offset in HEAD_OFFSETS:
         pl.semaphore_signal(barrier, inc=1, device_id=(head_peer(offset), pool), device_id_type=MESH)
 
+    lane = lax.broadcasted_iota(jnp.int32, (8, 128), 1)
+    inverse = jnp.ones((8, 128), F32)
+    for bit in range(6):
+        step = THETA ** (-2.0 * 2**bit / HD)
+        inverse = jnp.where((lane & (1 << bit)) != 0, inverse * step, inverse)
+
+    for copy in small:
+        copy.wait()
     slot_row = slot_ref[...]
     len_row = len_ref[...].astype(F32)
     to_slot = (lax.broadcasted_iota(jnp.int32, (64, 64), 0) == slot_row).astype(BF16)
     mine = pool * 4 + lax.broadcasted_iota(jnp.int32, (8, 64), 0) % 4
     lengths = jnp.sum(jnp.where(mine == slot_row, len_row, 0.0), axis=1, keepdims=True)
-    angle = lengths * inv_ref[...]
-    lane = lax.broadcasted_iota(jnp.int32, (8, 128), 1)
+    angle = lengths * inverse
     cosine = jnp.cos(angle)
     sine = jnp.where(lane < 64, -jnp.sin(angle), jnp.sin(angle))
 
@@ -259,16 +268,16 @@
 
 
 def local(hidden_in, w_query, w_key, w_value, w_out, k_cache, v_cache, cache_len, slot_of):
-    half = np.arange(128) % 64
-    inverse = np.broadcast_to((THETA ** (-2.0 * half / HD)).astype(np.float32)[None], (8, 128))
     hbm = pl.BlockSpec(memory_space=pl.ANY)
     vmem = pl.BlockSpec(memory_space=pltpu.VMEM)
     return pl.pallas_call(
         kernel,
         out_shape=jax.ShapeDtypeStruct((4, 1024), F32),
-        in_specs=[hbm] * 7 + [vmem] * 3,
+        in_specs=[hbm] * 9,
         out_specs=vmem,
         scratch_shapes=[
+            pltpu.VMEM((1, 64), jnp.int32),
+            pltpu.VMEM((1, 64), jnp.int32),
             pltpu.VMEM((64, 1024), BF16),
             pltpu.VMEM((1024, 1024), BF16),
             pltpu.VMEM((64, 1024), BF16),
@@ -292,17 +301,17 @@
             pltpu.VMEM((16, 32, 128), BF16),
             pltpu.VMEM((15, 32, 128), BF16),
             pltpu.VMEM((512, 512), BF16),
-            pltpu.SemaphoreType.DMA((10,)),
+            pltpu.SemaphoreType.DMA((12,)),
             pltpu.SemaphoreType.DMA((6,)),
             pltpu.SemaphoreType.DMA((6,)),
             pltpu.SemaphoreType.DMA((2,)),
         ],
         compiler_params=pltpu.CompilerParams(
-            collective_id=0, has_side_effects=True, vmem_limit_bytes=48 * 1024 * 1024
+            collective_id=0, has_side_effects=True, vmem_limit_bytes=63 * 1024 * 1024
         ),
     )(
         hidden_in, w_query, w_key.T, w_value.T, w_out, k_cache, v_cache,
-        cache_len.reshape(1, 64), slot_of.reshape(1, 64), jnp.asarray(inverse),
+        cache_len.reshape(1, 64), slot_of.reshape(1, 64),
     )
 
 

time: 50.6 us -> 43.3 us (0.86)
  local copies, waits for them, and re-layouts: 8.47 us -> 1.32 us
    unnamed x15 -> x1, local copies, waits for them, and re-layouts: 7.81 us -> 1.32 us
    another operation x1 -> x0, local copies, waits for them, and re-layouts: 0.66 us -> none
where the time goes in v2:
time: 43.3 us; the launch traced here: 43.1 us
  Pallas kernels  41.8 us (97%)
  local copies, waits for them, and re-layouts  1.32 us (3%)
    pallas_call x1, Pallas kernels, local(): pl.pallas_call(kernel, out_shape=jax.ShapeDtypeStruct((4, 1024), F32), in...  41.8 us
    unnamed x1, local copies, waits for them, and re-layouts  1.32 us

profile of v2, /device:TPU:1, one launch (start us, length us, event | category | flops | bytes accessed | tf_op | source)
XLA Modules:
  0.0 43.1 jit_solution(17548749944590640058)
XLA Ops:
  0.0 41.8 %shard_map.91 = f32[4,1024]{1,0:T(4,128)} custom-call(bf16[64,1024]{1,0:T(8,128)(2,1)} %hid_hbm.1, bf16[1024,1024]{1,0:T(8,128)(2,1)} %wq_hbm.1, bf16[64,1024]{1,0:T(8,128)(2,1)} %bitcast.4, bf16[64,1024]{1,0:T(8,128)(2,1)} %bitcast.5, bf16[1024,1024]{1,0:T(8,128)(2,1)} %wo_hbm.1, bf16[4,384,1024]{2,1,0:T(8,128)(2,1)} %k_hbm.1, bf16[4,384,1024]{2,1,0:T(8,128)(2,1)} %v_hbm.1, ...), custom_call_target="tpu_custom_call" | custom-call | tf_op jit(solution)/shard_map/pallas_call | solution.py:273
  41.8 1.3 %copy.11 = f32[4,1024]{1,0:T(4,128)} copy(f32[4,1024]{1,0:T(4,128)} %shard_map.91) | data formatting | bytes 32768

commit v3 on v2

v3 whole, which is shorter than its diff:
```python
import math

import jax
import jax.numpy as jnp
from jax import lax
from jax.experimental import pallas as pl
from jax.experimental.pallas import tpu as pltpu
from jax.sharding import PartitionSpec as P

QH = 128
KVH = 8
HD = 128
THETA = 500000.0
NEGATIVE = -1e30
MESH = pl.DeviceIdType.MESH
F32 = jnp.float32
BF16 = jnp.bfloat16
ACROSS = (((1,), (1,)), ((), ()))

POOL_OFFSETS = sorted(
    [(dy, dx) for dy in range(4) for dx in range(4) if (dy, dx) != (0, 0)],
    key=lambda o: -(min(o[0], 4 - o[0]) + min(o[1], 4 - o[1])),
)
HEAD_OFFSETS = sorted(
    [(dz, dc) for dz in range(8) for dc in range(2) if (dz, dc) != (0, 0)],
    key=lambda o: -(min(o[0], 8 - o[0]) + 0.5 * o[1]),
)

BATCHES = ((0, 1, 7), (2, 6), (3, 5), (4,))


def batch_of(dz):
    return next(i for i, steps in enumerate(BATCHES) if dz in steps)


def kernel(
    hid_hbm, wq_hbm, wk_hbm, wv_hbm, wo_hbm, k_hbm, v_hbm, len_hbm, slot_hbm, out_ref,
    len_ref, slot_ref, slot_smem, hid, wq, wkv, wo, kc, vc,
    s1, r1, skv, rkv, swap, s2, r2, s4, r4, st4, rt4, s5, r5, x5, x6, s6, r6,
    load_sem, send_sem, recv_sem, query_sem, swap_sem,
):
    head = lax.axis_index("head")
    pool = lax.axis_index("pool")
    z, core = head // 2, head % 2
    py, px = pool // 4, pool % 4

    def pool_peer(offset):
        return lax.rem(py + offset[0], 4) * 4 + lax.rem(px + offset[1], 4)

    def head_peer(offset):
        return lax.rem(z + offset[0], 8) * 2 + lax.rem(core + offset[1], 2)

    def pool_send(src, dst, phase, offset):
        pltpu.make_async_remote_copy(
            src, dst, send_sem.at[phase], recv_sem.at[phase],
            device_id=(head, pool_peer(offset)), device_id_type=MESH,
        ).start()

    def head_send(src, dst, phase, receive, offset):
        pltpu.make_async_remote_copy(
            src, dst, send_sem.at[phase], receive,
            device_id=(head_peer(offset), pool), device_id_type=MESH,
        ).start()

    def wait_bytes(view, sem):
        pltpu.make_async_copy(view, view, sem).wait()

    def first15(buf):
        return buf.at[pl.ds(0, 15)]

    loads = [
        pltpu.make_async_copy(slot_hbm, slot_ref, load_sem.at[0]),
        pltpu.make_async_copy(hid_hbm, hid, load_sem.at[1]),
    ]
    for c in range(2):
        cols = pl.ds(512 * c, 512)
        loads.append(pltpu.make_async_copy(wq_hbm.at[:, cols], wq.at[:, cols], load_sem.at[2 + c]))
    later = [
        pltpu.make_async_copy(wk_hbm, wkv.at[pl.ds(0, 64)], load_sem.at[6]),
        pltpu.make_async_copy(wv_hbm, wkv.at[pl.ds(64, 64)], load_sem.at[7]),
        pltpu.make_async_copy(len_hbm, len_ref, load_sem.at[8]),
        pltpu.make_async_copy(slot_hbm, slot_smem, load_sem.at[9]),
        pltpu.make_async_copy(k_hbm, kc, load_sem.at[10]),
        pltpu.make_async_copy(v_hbm, vc, load_sem.at[11]),
        pltpu.make_async_copy(wo_hbm, wo, load_sem.at[12]),
    ]
    barrier = pltpu.get_barrier_semaphore()
    for offset in POOL_OFFSETS:
        pl.semaphore_signal(barrier, inc=1, device_id=(head, pool_peer(offset)), device_id_type=MESH)
    for copy in loads:
        copy.start()
    for offset in HEAD_OFFSETS:
        pl.semaphore_signal(barrier, inc=1, device_id=(head_peer(offset), pool), device_id_type=MESH)

    loads[0].wait()
    slot_row = slot_ref[...]
    to_slot = (lax.broadcasted_iota(jnp.int32, (64, 64), 0) == slot_row).astype(BF16)
    loads[1].wait()
    hidden = jnp.dot(to_slot, hid[...], preferred_element_type=F32).astype(BF16)
    for c in range(2):
        loads[2 + c].wait()
        if c == 1:
            for copy in later:
                copy.start()
        part = jnp.dot(hidden, wq[:, 512 * c : 512 * c + 512], preferred_element_type=F32)
        for j in range(4):
            s1[pl.ds(4 * c + j, 64, stride=8), :] = part[:, 128 * j : 128 * j + 128]
    pl.semaphore_wait(barrier, 30)
    for i, offset in enumerate(POOL_OFFSETS):
        rows = pl.ds(pl.multiple_of(32 * pool_peer(offset), 32), 32)
        pool_send(s1.at[rows], r1.at[i], 0, offset)

    later[0].wait()
    later[1].wait()
    key_value = lax.dot_general(hidden, wkv[...], ACROSS, preferred_element_type=F32)
    for p in range(16):
        skv[p] = key_value[4 * p : 4 * p + 4]
    for i, offset in enumerate(POOL_OFFSETS):
        pool_send(skv.at[pool_peer(offset)], rkv.at[i], 1, offset)

    later[2].wait()
    lane = lax.broadcasted_iota(jnp.int32, (8, 128), 1)
    inverse = jnp.ones((8, 128), F32)
    for bit in range(6):
        step = THETA ** (-2.0 * 2**bit / HD)
        inverse = jnp.where((lane & (1 << bit)) != 0, inverse * step, inverse)
    mine = pool * 4 + lax.broadcasted_iota(jnp.int32, (8, 64), 0) % 4
    lengths = jnp.sum(jnp.where(mine == slot_row, len_ref[...].astype(F32), 0.0), axis=1, keepdims=True)
    angle = lengths * inverse
    cosine = jnp.cos(angle)
    sine = jnp.where(lane < 64, -jnp.sin(angle), jnp.sin(angle))

    def rotate(x, rows):
        return x * cosine[rows] + pltpu.roll(x, 64, 1) * sine[rows]

    wait_bytes(r1, recv_sem.at[0])
    total = s1[pl.ds(pl.multiple_of(32 * pool, 32), 32), :]
    for i in range(15):
        total = total + r1[i]

    query = jnp.concatenate(
        [rotate(total[8 * s : 8 * s + 8], slice(s, s + 1)) for s in range(4)], axis=0
    ).astype(BF16)
    s2[...] = query
    for offset in HEAD_OFFSETS[::-1]:
        head_send(s2, r2.at[offset[0], core], 2, query_sem.at[batch_of(offset[0])], offset)
    r2[0, core] = query

    wait_bytes(rkv, recv_sem.at[1])
    here = skv[pool]
    for i in range(15):
        here = here + rkv[i]
    swap[0] = here
    swap_copy = pltpu.make_async_remote_copy(
        swap.at[0], swap.at[1], swap_sem.at[0], swap_sem.at[1],
        device_id=(z * 2 + 1 - core, pool), device_id_type=MESH,
    )
    swap_copy.start()

    scale = 1.0 / math.sqrt(HD)
    later[4].wait()
    later[5].wait()
    place = (head * 384 + lax.broadcasted_iota(jnp.int32, (1, 384), 1)).astype(F32)
    valid = [jnp.broadcast_to(place < lengths[s : s + 1, :], (16, 384)) for s in range(4)]
    row32 = lax.broadcasted_iota(jnp.int32, (32, 128), 0)
    lane32 = lax.broadcasted_iota(jnp.int32, (32, 128), 1)
    for batch, steps in enumerate(BATCHES):
        messages = sum(2 for dz in steps if dz) + (1 if 0 in steps else 0)
        wait_bytes(r4.at[pl.ds(0, messages)], query_sem.at[batch])
        pairs = [(dz, s) for dz in steps for s in range(4)]
        cols = {dz: pl.ds(pl.multiple_of(lax.rem(z + dz, 8) * 128, 128), 128) for dz in steps}
        arrived = {dz: r2[(8 - dz) % 8].astype(F32).reshape(2, 4, 8, 128) for dz in steps}
        scores = [
            lax.dot_general(
                arrived[dz][:, s].reshape(16, 128).astype(BF16), kc[s, :, cols[dz]], ACROSS,
                preferred_element_type=F32,
            ) * scale
            for dz, s in pairs
        ]
        tops = [
            jnp.max(jnp.where(valid[s], x, NEGATIVE), axis=1, keepdims=True)
            for x, (_, s) in zip(scores, pairs)
        ]
        weights = [
            jnp.where(valid[s], jnp.exp(x - top), 0.0) for x, top, (_, s) in zip(scores, tops, pairs)
        ]
        bottoms = [jnp.sum(x, axis=1, keepdims=True) for x in weights]
        sums = [
            jnp.dot(x.astype(BF16), vc[s, :, cols[dz]], preferred_element_type=F32)
            for x, (dz, s) in zip(weights, pairs)
        ]
        for i, dz in enumerate(steps):
            mine = slice(4 * i, 4 * i + 4)
            for c in range(2):
                half = slice(8 * c, 8 * c + 8)
                top = jnp.concatenate([x[half] for x in tops[mine]], axis=0)
                bottom = jnp.concatenate([x[half] for x in bottoms[mine]], axis=0)
                row = jnp.where(row32 == lane32, top, 0.0) + jnp.where(row32 + 32 == lane32, bottom, 0.0)
                st4[dz, c] = jnp.sum(row, axis=0, keepdims=True)
                s4[dz, c] = jnp.concatenate([x[half] for x in sums[mine]], axis=0).astype(BF16)
        for dz in steps:
            for dc in range(2):
                to = lax.rem(core + dc, 2)
                if dz or dc:
                    slot = 2 * dz + dc - 1
                    head_send(st4.at[dz, to], rt4.at[slot], 3, recv_sem.at[3], (dz, dc))
                    head_send(s4.at[dz, to], r4.at[slot], 4, recv_sem.at[4], (dz, dc))
    swap_copy.wait()
    there = swap[1]
    lane4 = lax.broadcasted_iota(jnp.int32, (4, 128), 1)
    here_turned, there_turned = pltpu.roll(here, 64, 1), pltpu.roll(there, 64, 1)
    first = core == 0
    key_raw = jnp.where(lane4 < 64, jnp.where(first, here, there), jnp.where(first, there_turned, here_turned))
    value_raw = jnp.where(lane4 < 64, jnp.where(first, here_turned, there_turned), jnp.where(first, there, here))
    key_new = rotate(key_raw, slice(0, 4)).astype(BF16).astype(F32)
    value_new = value_raw.astype(BF16).astype(F32)

    def spread(x):
        return jnp.concatenate([jnp.broadcast_to(x[s : s + 1], (8, 128)) for s in range(4)], axis=0)

    own = jnp.sum(query.astype(F32) * spread(key_new), axis=1, keepdims=True) * scale
    own = jnp.sum(jnp.where(row32 == lane32, own, 0.0), axis=0, keepdims=True)

    wait_bytes(rt4, recv_sem.at[3])
    parts = jnp.concatenate([rt4[i] for i in range(15)] + [st4[0, core]], axis=0)
    largest = jnp.maximum(jnp.max(parts, axis=0, keepdims=True), own)
    factor = jnp.exp(parts - largest)
    own_weight = jnp.exp(own - largest)
    denominator = jnp.sum(factor * pltpu.roll(parts, 96, 1), axis=0, keepdims=True) + own_weight
    shares = jnp.concatenate(
        [factor / denominator, own_weight.astype(BF16).astype(F32) / denominator, jnp.zeros((111, 128), F32)], axis=0
    ).T
    attention = shares[:32, 16:17] * spread(value_new)
    wait_bytes(r4, recv_sem.at[4])
    for i in range(16):
        part = r4[i] if i < 15 else s4[0, core]
        attention = attention + shares[:32, i : i + 1] * part.astype(F32)
    attention = attention.astype(BF16)

    s5[...] = attention
    for i, offset in enumerate(POOL_OFFSETS):
        pool_send(s5, r5.at[pool], 5, offset)
    r5[pool] = attention
    later[3].wait()
    later[6].wait()
    wait_bytes(first15(r5), recv_sem.at[5])
    x5[...] = r5[...].astype(F32).reshape(512, 128)
    rows = jnp.concatenate([x5[pl.ds(j, 64, stride=8), :].astype(BF16) for j in range(8)], axis=1)

    for c in range(4):
        part = jnp.dot(rows, wo[:, 256 * c : 256 * c + 256], preferred_element_type=F32)
        x6[:, 2 * c, :] = part[:, :128]
        x6[:, 2 * c + 1, :] = part[:, 128:]
    for r in range(0, 64, 2):
        pair = [x6[slot_smem[0, r + i]] for i in range(2)]
        s6[r // 4, 8 * (r % 4) : 8 * (r % 4) + 16, :] = jnp.concatenate(pair, axis=0).astype(BF16)
    for i, offset in enumerate(HEAD_OFFSETS):
        head_send(s6.at[head_peer(offset)], r6.at[i], 6, recv_sem.at[6], offset)
    wait_bytes(r6, recv_sem.at[6])
    mixed = s6[head].astype(F32)
    for i in range(15):
        mixed = mixed + r6[i].astype(F32)
    out_ref[...] = mixed

    wait_bytes(r1, send_sem.at[0])
    wait_bytes(rkv, send_sem.at[1])
    wait_bytes(r4, send_sem.at[2])
    wait_bytes(rt4, send_sem.at[3])
    wait_bytes(r4, send_sem.at[4])
    wait_bytes(first15(r5), send_sem.at[5])
    wait_bytes(r6, send_sem.at[6])


def local(hidden_in, w_query, w_key, w_value, w_out, k_cache, v_cache, cache_len, slot_of):
    hbm = pl.BlockSpec(memory_space=pl.ANY)
    vmem = pl.BlockSpec(memory_space=pltpu.VMEM)
    return pl.pallas_call(
        kernel,
        out_shape=jax.ShapeDtypeStruct((32, 128), F32),
        in_specs=[hbm] * 9,
        out_specs=vmem,
        scratch_shapes=[
            pltpu.VMEM((1, 64), jnp.int32),
            pltpu.VMEM((1, 64), jnp.int32),
            pltpu.SMEM((1, 64), jnp.int32),
            pltpu.VMEM((64, 1024), BF16),
            pltpu.VMEM((1024, 1024), BF16),
            pltpu.VMEM((128, 1024), BF16),
            pltpu.VMEM((1024, 1024), BF16),
            pltpu.VMEM((4, 384, 1024), BF16),
            pltpu.VMEM((4, 384, 1024), BF16),
            pltpu.VMEM((512, 128), F32),
            pltpu.VMEM((15, 32, 128), F32),
            pltpu.VMEM((16, 4, 128), F32),
            pltpu.VMEM((15, 4, 128), F32),
            pltpu.VMEM((2, 4, 128), F32),
            pltpu.VMEM((32, 128), BF16),
            pltpu.VMEM((8, 2, 32, 128), BF16),
            pltpu.VMEM((8, 2, 32, 128), BF16),
            pltpu.VMEM((15, 32, 128), BF16),
            pltpu.VMEM((8, 2, 1, 128), F32),
            pltpu.VMEM((15, 1, 128), F32),
            pltpu.VMEM((32, 128), BF16),
            pltpu.VMEM((16, 32, 128), BF16),
            pltpu.VMEM((512, 128), F32),
            pltpu.VMEM((64, 8, 128), F32),
            pltpu.VMEM((16, 32, 128), BF16),
            pltpu.VMEM((15, 32, 128), BF16),
            pltpu.SemaphoreType.DMA((13,)),
            pltpu.SemaphoreType.DMA((7,)),
            pltpu.SemaphoreType.DMA((7,)),
            pltpu.SemaphoreType.DMA((4,)),
            pltpu.SemaphoreType.DMA((2,)),
        ],
        compiler_params=pltpu.CompilerParams(
            collective_id=0, has_side_effects=True, vmem_limit_bytes=63 * 1024 * 1024
        ),
    )(
        hidden_in, w_query, w_key.T, w_value.T, w_out, k_cache, v_cache,
        cache_len.reshape(1, 64), slot_of.reshape(1, 64),
    ).reshape(4, 1024)


def solution(mesh):
    in_specs = (
        P(None, "pool"),
        P("pool", "head"),
        P("pool", "head"),
        P("pool", "head"),
        P("head", "pool"),
        P("pool", "head", None),
        P("pool", "head", None),
        P(),
        P(),
    )
    out_specs = P("head", "pool")
    return jax.shard_map(local, mesh=mesh, in_specs=in_specs, out_specs=out_specs, check_vma=False)
```

time: 43.3 us -> 41 us (0.947)
  Pallas kernels: 41.8 us -> 39.5 us
    pallas_call x1, Pallas kernels: 41.8 us -> 39.5 us  [local(): pl.pallas_call(kernel, out_shape=jax.ShapeDtypeStruct((32, 128), F32), in...]
    reshape x0 -> x1, local copies, waits for them, and re-layouts: none -> 1.33 us  [local(): return pl.pallas_call(kernel, out_shape=jax.ShapeDtypeStruct((32, 128), F...]
    unnamed x1 -> x0, local copies, waits for them, and re-layouts: 1.32 us -> none
where the time goes in v3:
time: 41 us; the launch traced here: 40.9 us
  Pallas kernels  39.5 us (96%)
  local copies, waits for them, and re-layouts  1.33 us (3%)
    pallas_call x1, Pallas kernels, local(): pl.pallas_call(kernel, out_shape=jax.ShapeDtypeStruct((32, 128), F32), in...  39.5 us
    reshape x1, local copies, waits for them, and re-layouts, local(): return pl.pallas_call(kernel, out_shape=jax.ShapeDtypeStruct((32, 128), F...  1.33 us

profile of v3, /device:TPU:1, one launch (start us, length us, event | category | flops | bytes accessed | tf_op | source)
XLA Modules:
  0.0 40.9 jit_solution(17499135396889616143)
XLA Ops:
  0.0 39.5 %shard_map.91 = f32[32,128]{1,0:T(8,128)} custom-call(bf16[64,1024]{1,0:T(8,128)(2,1)} %hid_hbm.1, bf16[1024,1024]{1,0:T(8,128)(2,1)} %wq_hbm.1, bf16[64,1024]{1,0:T(8,128)(2,1)} %bitcast.4, bf16[64,1024]{1,0:T(8,128)(2,1)} %bitcast.5, bf16[1024,1024]{1,0:T(8,128)(2,1)} %wo_hbm.1, bf16[4,384,1024]{2,1,0:T(8,128)(2,1)} %k_hbm.1, bf16[4,384,1024]{2,1,0:T(8,128)(2,1)} %v_hbm.1, ...), custom_call_target="tpu_custom_call" | custom-call | tf_op jit(solution)/shard_map/pallas_call | solution.py:277
  39.5 1.3 %reshape.11 = f32[4,1024]{1,0:T(4,128)} reshape(f32[32,128]{1,0:T(8,128)} %shard_map.91) | data formatting | bytes 32768 | tf_op jit(solution)/shard_map/reshape | solution.py:321

commit v4 on v3

--- a/solution.py
+++ b/solution.py
@@ -26,18 +26,19 @@
     key=lambda o: -(min(o[0], 8 - o[0]) + 0.5 * o[1]),
 )
 
-BATCHES = ((0, 1, 7), (2, 6), (3, 5), (4,))
-
-
-def batch_of(dz):
-    return next(i for i, steps in enumerate(BATCHES) if dz in steps)
+BATCHES = ((0,), (3,), (1,), (2,))
+CHIP_OFFSETS = (1, 7, 2, 6, 3, 5, 4, 0)
+
+
+def group_slot(dz):
+    return ((8 - dz) % 8 - dz % 2) // 2
 
 
 def kernel(
     hid_hbm, wq_hbm, wk_hbm, wv_hbm, wo_hbm, k_hbm, v_hbm, len_hbm, slot_hbm, out_ref,
     len_ref, slot_ref, slot_smem, hid, wq, wkv, wo, kc, vc,
     s1, r1, skv, rkv, swap, s2, r2, s4, r4, st4, rt4, s5, r5, x5, x6, s6, r6,
-    load_sem, send_sem, recv_sem, query_sem, swap_sem,
+    load_sem, send_sem, recv_sem, query_sem, swap_sem, cache_sem,
 ):
     head = lax.axis_index("head")
     pool = lax.axis_index("pool")
@@ -80,10 +81,27 @@
         pltpu.make_async_copy(wv_hbm, wkv.at[pl.ds(64, 64)], load_sem.at[7]),
         pltpu.make_async_copy(len_hbm, len_ref, load_sem.at[8]),
         pltpu.make_async_copy(slot_hbm, slot_smem, load_sem.at[9]),
-        pltpu.make_async_copy(k_hbm, kc, load_sem.at[10]),
-        pltpu.make_async_copy(v_hbm, vc, load_sem.at[11]),
-        pltpu.make_async_copy(wo_hbm, wo, load_sem.at[12]),
     ]
+    last = pltpu.make_async_copy(wo_hbm, wo, load_sem.at[10])
+
+    def group_lanes(owner, i):
+        return pl.ds(pl.multiple_of(lax.rem(z + owner + 2 * i, 8) * 128, 128), 128)
+
+    kept, given = [], []
+    for n, (source, cache) in enumerate(((k_hbm, kc), (v_hbm, vc))):
+        for i in range(4):
+            kept.append(
+                pltpu.make_async_copy(
+                    source.at[:, :, group_lanes(core, i)], cache.at[i, core], cache_sem.at[0, 4 * n + i]
+                )
+            )
+            given.append(
+                pltpu.make_async_remote_copy(
+                    source.at[:, :, group_lanes(1 - core, i)], cache.at[i, core],
+                    cache_sem.at[1, 4 * n + i], cache_sem.at[2, 4 * n + i],
+                    device_id=(z * 2 + 1 - core, pool), device_id_type=MESH,
+                )
+            )
     barrier = pltpu.get_barrier_semaphore()
     for offset in POOL_OFFSETS:
         pl.semaphore_signal(barrier, inc=1, device_id=(head, pool_peer(offset)), device_id_type=MESH)
@@ -100,7 +118,7 @@
     for c in range(2):
         loads[2 + c].wait()
         if c == 1:
-            for copy in later:
+            for copy in later + kept + [last]:
                 copy.start()
         part = jnp.dot(hidden, wq[:, 512 * c : 512 * c + 512], preferred_element_type=F32)
         for j in range(4):
@@ -109,6 +127,8 @@
     for i, offset in enumerate(POOL_OFFSETS):
         rows = pl.ds(pl.multiple_of(32 * pool_peer(offset), 32), 32)
         pool_send(s1.at[rows], r1.at[i], 0, offset)
+    for copy in given[:4]:
+        copy.start()
 
     later[0].wait()
     later[1].wait()
@@ -117,6 +137,8 @@
         skv[p] = key_value[4 * p : 4 * p + 4]
     for i, offset in enumerate(POOL_OFFSETS):
         pool_send(skv.at[pool_peer(offset)], rkv.at[i], 1, offset)
+    for copy in given[4:]:
+        copy.start()
 
     later[2].wait()
     lane = lax.broadcasted_iota(jnp.int32, (8, 128), 1)
@@ -142,9 +164,20 @@
         [rotate(total[8 * s : 8 * s + 8], slice(s, s + 1)) for s in range(4)], axis=0
     ).astype(BF16)
     s2[...] = query
-    for offset in HEAD_OFFSETS[::-1]:
-        head_send(s2, r2.at[offset[0], core], 2, query_sem.at[batch_of(offset[0])], offset)
-    r2[0, core] = query
+    for dz in CHIP_OFFSETS[:-1]:
+        i = group_slot(dz)
+        pltpu.make_async_remote_copy(
+            s2, r2.at[i, core], send_sem.at[2], query_sem.at[i],
+            device_id=(lax.rem(z + dz, 8) * 2 + dz % 2, pool), device_id_type=MESH,
+        ).start()
+
+    @pl.when(core == 0)
+    def _():
+        pltpu.make_async_copy(s2, r2.at[0, 0], query_sem.at[0]).start()
+
+    @pl.when(core == 1)
+    def _():
+        head_send(s2, r2.at[0, 1], 2, query_sem.at[0], (0, 1))
 
     wait_bytes(rkv, recv_sem.at[1])
     here = skv[pool]
@@ -158,24 +191,24 @@
     swap_copy.start()
 
     scale = 1.0 / math.sqrt(HD)
-    later[4].wait()
-    later[5].wait()
-    place = (head * 384 + lax.broadcasted_iota(jnp.int32, (1, 384), 1)).astype(F32)
-    valid = [jnp.broadcast_to(place < lengths[s : s + 1, :], (16, 384)) for s in range(4)]
+    place = (z * 768 + lax.broadcasted_iota(jnp.int32, (1, 768), 1)).astype(F32)
+    valid = [jnp.broadcast_to(place < lengths[s : s + 1, :], (16, 768)) for s in range(4)]
     row32 = lax.broadcasted_iota(jnp.int32, (32, 128), 0)
     lane32 = lax.broadcasted_iota(jnp.int32, (32, 128), 1)
-    for batch, steps in enumerate(BATCHES):
-        messages = sum(2 for dz in steps if dz) + (1 if 0 in steps else 0)
-        wait_bytes(r4.at[pl.ds(0, messages)], query_sem.at[batch])
-        pairs = [(dz, s) for dz in steps for s in range(4)]
-        cols = {dz: pl.ds(pl.multiple_of(lax.rem(z + dz, 8) * 128, 128), 128) for dz in steps}
-        arrived = {dz: r2[(8 - dz) % 8].astype(F32).reshape(2, 4, 8, 128) for dz in steps}
+    for batch in BATCHES:
+        for i in batch:
+            wait_bytes(r2.at[i], query_sem.at[i])
+            for n in (i, 4 + i):
+                kept[n].wait()
+                given[n].wait_recv()
+        pairs = [(i, s) for i in batch for s in range(4)]
+        arrived = {i: r2[i].astype(F32).reshape(2, 4, 8, 128) for i in batch}
+        queries = [arrived[i][:, s].reshape(16, 128).astype(BF16) for i, s in pairs]
         scores = [
-            lax.dot_general(
-                arrived[dz][:, s].reshape(16, 128).astype(BF16), kc[s, :, cols[dz]], ACROSS,
-                preferred_element_type=F32,
+            jnp.concatenate(
+                [lax.dot_general(q, kc[i, c, s], ACROSS, preferred_element_type=F32) for c in range(2)], axis=1
             ) * scale
-            for dz, s in pairs
+            for q, (i, s) in zip(queries, pairs)
         ]
         tops = [
             jnp.max(jnp.where(valid[s], x, NEGATIVE), axis=1, keepdims=True)
@@ -185,26 +218,47 @@
             jnp.where(valid[s], jnp.exp(x - top), 0.0) for x, top, (_, s) in zip(scores, tops, pairs)
         ]
         bottoms = [jnp.sum(x, axis=1, keepdims=True) for x in weights]
+        weights = [x.astype(BF16) for x in weights]
         sums = [
-            jnp.dot(x.astype(BF16), vc[s, :, cols[dz]], preferred_element_type=F32)
-            for x, (dz, s) in zip(weights, pairs)
+            jnp.dot(x[:, :384], vc[i, 0, s], preferred_element_type=F32)
+            + jnp.dot(x[:, 384:], vc[i, 1, s], preferred_element_type=F32)
+            for x, (i, s) in zip(weights, pairs)
         ]
-        for i, dz in enumerate(steps):
-            mine = slice(4 * i, 4 * i + 4)
+        for n, i in enumerate(batch):
+            mine = slice(4 * n, 4 * n + 4)
             for c in range(2):
                 half = slice(8 * c, 8 * c + 8)
                 top = jnp.concatenate([x[half] for x in tops[mine]], axis=0)
                 bottom = jnp.concatenate([x[half] for x in bottoms[mine]], axis=0)
                 row = jnp.where(row32 == lane32, top, 0.0) + jnp.where(row32 + 32 == lane32, bottom, 0.0)
-                st4[dz, c] = jnp.sum(row, axis=0, keepdims=True)
-                s4[dz, c] = jnp.concatenate([x[half] for x in sums[mine]], axis=0).astype(BF16)
-        for dz in steps:
-            for dc in range(2):
-                to = lax.rem(core + dc, 2)
-                if dz or dc:
-                    slot = 2 * dz + dc - 1
-                    head_send(st4.at[dz, to], rt4.at[slot], 3, recv_sem.at[3], (dz, dc))
-                    head_send(s4.at[dz, to], r4.at[slot], 4, recv_sem.at[4], (dz, dc))
+                st4[i, c] = jnp.sum(row, axis=0, keepdims=True)
+                s4[i, c] = jnp.concatenate([x[half] for x in sums[mine]], axis=0).astype(BF16)
+        for i in batch:
+            chip = lax.rem(z + core + 2 * i, 8)
+            slot = lax.rem(8 - core - 2 * i + 8, 8)
+            for c in range(2):
+                remote = [
+                    pltpu.make_async_remote_copy(
+                        src.at[i, c], dst.at[slot], send_sem.at[phase], recv_sem.at[phase],
+                        device_id=(chip * 2 + c, pool), device_id_type=MESH,
+                    )
+                    for src, dst, phase in ((st4, rt4, 3), (s4, r4, 4))
+                ]
+                if i or c:
+                    for copy in remote:
+                        copy.start()
+                else:
+
+                    @pl.when(core == 1)
+                    def _(remote=remote):
+                        for copy in remote:
+                            copy.start()
+
+                    @pl.when(core == 0)
+                    def _():
+                        pltpu.make_async_copy(st4.at[0, 0], rt4.at[0], recv_sem.at[3]).start()
+                        pltpu.make_async_copy(s4.at[0, 0], r4.at[0], recv_sem.at[4]).start()
+
     swap_copy.wait()
     there = swap[1]
     lane4 = lax.broadcasted_iota(jnp.int32, (4, 128), 1)
@@ -222,19 +276,18 @@
     own = jnp.sum(jnp.where(row32 == lane32, own, 0.0), axis=0, keepdims=True)
 
     wait_bytes(rt4, recv_sem.at[3])
-    parts = jnp.concatenate([rt4[i] for i in range(15)] + [st4[0, core]], axis=0)
+    parts = jnp.concatenate([rt4[i] for i in range(8)], axis=0)
     largest = jnp.maximum(jnp.max(parts, axis=0, keepdims=True), own)
     factor = jnp.exp(parts - largest)
     own_weight = jnp.exp(own - largest)
     denominator = jnp.sum(factor * pltpu.roll(parts, 96, 1), axis=0, keepdims=True) + own_weight
     shares = jnp.concatenate(
-        [factor / denominator, own_weight.astype(BF16).astype(F32) / denominator, jnp.zeros((111, 128), F32)], axis=0
+        [factor / denominator, own_weight.astype(BF16).astype(F32) / denominator, jnp.zeros((119, 128), F32)], axis=0
     ).T
-    attention = shares[:32, 16:17] * spread(value_new)
+    attention = shares[:32, 8:9] * spread(value_new)
     wait_bytes(r4, recv_sem.at[4])
-    for i in range(16):
-        part = r4[i] if i < 15 else s4[0, core]
-        attention = attention + shares[:32, i : i + 1] * part.astype(F32)
+    for i in range(8):
+        attention = attention + shares[:32, i : i + 1] * r4[i].astype(F32)
     attention = attention.astype(BF16)
 
     s5[...] = attention
@@ -242,7 +295,7 @@
         pool_send(s5, r5.at[pool], 5, offset)
     r5[pool] = attention
     later[3].wait()
-    later[6].wait()
+    last.wait()
     wait_bytes(first15(r5), recv_sem.at[5])
     x5[...] = r5[...].astype(F32).reshape(512, 128)
     rows = jnp.concatenate([x5[pl.ds(j, 64, stride=8), :].astype(BF16) for j in range(8)], axis=1)
@@ -264,9 +317,15 @@
 
     wait_bytes(r1, send_sem.at[0])
     wait_bytes(rkv, send_sem.at[1])
-    wait_bytes(r4, send_sem.at[2])
-    wait_bytes(rt4, send_sem.at[3])
-    wait_bytes(r4, send_sem.at[4])
+    for copy in given:
+        copy.wait_send()
+    for buf, phase in ((r4, 2), (rt4, 3), (r4, 4)):
+        wait_bytes(buf.at[pl.ds(0, 7)], send_sem.at[phase])
+
+        @pl.when(core == 1)
+        def _(buf=buf, phase=phase):
+            wait_bytes(buf.at[0], send_sem.at[phase])
+
     wait_bytes(first15(r5), send_sem.at[5])
     wait_bytes(r6, send_sem.at[6])
 
@@ -276,7 +335,7 @@
     vmem = pl.BlockSpec(memory_space=pltpu.VMEM)
     return pl.pallas_call(
         kernel,
-        out_shape=jax.ShapeDtypeStruct((32, 128), F32),
+        out_shape=pltpu.VMEM((32, 128), F32),
         in_specs=[hbm] * 9,
         out_specs=vmem,
         scratch_shapes=[
@@ -287,30 +346,31 @@
             pltpu.VMEM((1024, 1024), BF16),
             pltpu.VMEM((128, 1024), BF16),
             pltpu.VMEM((1024, 1024), BF16),
-            pltpu.VMEM((4, 384, 1024), BF16),
-            pltpu.VMEM((4, 384, 1024), BF16),
+            pltpu.VMEM((4, 2, 4, 384, 128), BF16),
+            pltpu.VMEM((4, 2, 4, 384, 128), BF16),
             pltpu.VMEM((512, 128), F32),
             pltpu.VMEM((15, 32, 128), F32),
             pltpu.VMEM((16, 4, 128), F32),
             pltpu.VMEM((15, 4, 128), F32),
             pltpu.VMEM((2, 4, 128), F32),
             pltpu.VMEM((32, 128), BF16),
-            pltpu.VMEM((8, 2, 32, 128), BF16),
-            pltpu.VMEM((8, 2, 32, 128), BF16),
-            pltpu.VMEM((15, 32, 128), BF16),
-            pltpu.VMEM((8, 2, 1, 128), F32),
-            pltpu.VMEM((15, 1, 128), F32),
+            pltpu.VMEM((4, 2, 32, 128), BF16),
+            pltpu.VMEM((4, 2, 32, 128), BF16),
+            pltpu.VMEM((8, 32, 128), BF16),
+            pltpu.VMEM((4, 2, 1, 128), F32),
+            pltpu.VMEM((8, 1, 128), F32),
             pltpu.VMEM((32, 128), BF16),
             pltpu.VMEM((16, 32, 128), BF16),
             pltpu.VMEM((512, 128), F32),
             pltpu.VMEM((64, 8, 128), F32),
             pltpu.VMEM((16, 32, 128), BF16),
             pltpu.VMEM((15, 32, 128), BF16),
-            pltpu.SemaphoreType.DMA((13,)),
+            pltpu.SemaphoreType.DMA((11,)),
             pltpu.SemaphoreType.DMA((7,)),
             pltpu.SemaphoreType.DMA((7,)),
             pltpu.SemaphoreType.DMA((4,)),
             pltpu.SemaphoreType.DMA((2,)),
+            pltpu.SemaphoreType.DMA((3, 8)),
         ],
         compiler_params=pltpu.CompilerParams(
             collective_id=0, has_side_effects=True, vmem_limit_bytes=63 * 1024 * 1024

time: 41 us -> 38.9 us (0.949)
  Pallas kernels: 39.5 us -> 38.2 us
  local copies, waits for them, and re-layouts: 1.33 us -> 0.62 us
    pallas_call x1, Pallas kernels: 39.5 us -> 38.2 us  [local(): pl.pallas_call(kernel, out_shape=pltpu.VMEM((32, 128), F32), in_specs=[hb...]
    reshape x1, local copies, waits for them, and re-layouts: 1.33 us -> 0.62 us  [local(): return pl.pallas_call(kernel, out_shape=pltpu.VMEM((32, 128), F32), in_sp...]
where the time goes in v4:
time: 38.9 us; the launch traced here: 38.8 us
  Pallas kernels  38.2 us (98%)
  local copies, waits for them, and re-layouts  0.62 us (2%)
    pallas_call x1, Pallas kernels, local(): pl.pallas_call(kernel, out_shape=pltpu.VMEM((32, 128), F32), in_specs=[hb...  38.2 us

profile of v4, /device:TPU:1, one launch (start us, length us, event | category | flops | bytes accessed | tf_op | source)
XLA Modules:
  0.0 38.8 jit_solution(537195197604888736)
XLA Ops:
  0.0 38.2 %shard_map.91 = f32[32,128]{1,0:T(8,128)S(1)} custom-call(bf16[64,1024]{1,0:T(8,128)(2,1)} %hid_hbm.1, bf16[1024,1024]{1,0:T(8,128)(2,1)} %wq_hbm.1, bf16[64,1024]{1,0:T(8,128)(2,1)} %bitcast.4, bf16[64,1024]{1,0:T(8,128)(2,1)} %bitcast.5, bf16[1024,1024]{1,0:T(8,128)(2,1)} %wo_hbm.1, bf16[4,384,1024]{2,1,0:T(8,128)(2,1)} %k_hbm.1, ...), custom_call_target="tpu_custom_call" | custom-call | tf_op jit(solution)/shard_map/pallas_call | solution.py:336
  38.2 0.6 %reshape.11 = f32[4,1024]{1,0:T(4,128)} reshape(f32[32,128]{1,0:T(8,128)S(1)} %shard_map.91) | data formatting | bytes 32768 | tf_op jit(solution)/shard_map/reshape | solution.py:381

commit v5 on v4

--- a/solution.py
+++ b/solution.py
@@ -21,13 +21,18 @@
     [(dy, dx) for dy in range(4) for dx in range(4) if (dy, dx) != (0, 0)],
     key=lambda o: -(min(o[0], 4 - o[0]) + min(o[1], 4 - o[1])),
 )
+FAR_ROWS = 5
 HEAD_OFFSETS = sorted(
     [(dz, dc) for dz in range(8) for dc in range(2) if (dz, dc) != (0, 0)],
     key=lambda o: -(min(o[0], 8 - o[0]) + 0.5 * o[1]),
 )
+OUTPUT_OFFSETS = sorted(
+    HEAD_OFFSETS, key=lambda o: (min(o[0], 8 - o[0]) < 3, -o[1], -min(o[0], 8 - o[0]))
+) + [(0, 0)]
+FAR_OUTPUTS = 6
 
 BATCHES = ((0,), (3,), (1,), (2,))
-CHIP_OFFSETS = (1, 7, 2, 6, 3, 5, 4, 0)
+CHIP_OFFSETS = (3, 5, 4, 1, 7, 2, 6, 0)
 
 
 def group_slot(dz):
@@ -65,9 +70,6 @@
 
     def wait_bytes(view, sem):
         pltpu.make_async_copy(view, view, sem).wait()
-
-    def first15(buf):
-        return buf.at[pl.ds(0, 15)]
 
     loads = [
         pltpu.make_async_copy(slot_hbm, slot_ref, load_sem.at[0]),
@@ -135,8 +137,6 @@
     key_value = lax.dot_general(hidden, wkv[...], ACROSS, preferred_element_type=F32)
     for p in range(16):
         skv[p] = key_value[4 * p : 4 * p + 4]
-    for i, offset in enumerate(POOL_OFFSETS):
-        pool_send(skv.at[pool_peer(offset)], rkv.at[i], 1, offset)
     for copy in given[4:]:
         copy.start()
 
@@ -179,16 +179,8 @@
     def _():
         head_send(s2, r2.at[0, 1], 2, query_sem.at[0], (0, 1))
 
-    wait_bytes(rkv, recv_sem.at[1])
-    here = skv[pool]
-    for i in range(15):
-        here = here + rkv[i]
-    swap[0] = here
-    swap_copy = pltpu.make_async_remote_copy(
-        swap.at[0], swap.at[1], swap_sem.at[0], swap_sem.at[1],
-        device_id=(z * 2 + 1 - core, pool), device_id_type=MESH,
-    )
-    swap_copy.start()
+    for i, offset in enumerate(POOL_OFFSETS):
+        pool_send(skv.at[pool_peer(offset)], rkv.at[i], 1, offset)
 
     scale = 1.0 / math.sqrt(HD)
     place = (z * 768 + lax.broadcasted_iota(jnp.int32, (1, 768), 1)).astype(F32)
@@ -196,6 +188,17 @@
     row32 = lax.broadcasted_iota(jnp.int32, (32, 128), 0)
     lane32 = lax.broadcasted_iota(jnp.int32, (32, 128), 1)
     for batch in BATCHES:
+        if batch == BATCHES[-1]:
+            wait_bytes(rkv, recv_sem.at[1])
+            here = skv[pool]
+            for i in range(15):
+                here = here + rkv[i]
+            swap[0] = here
+            swap_copy = pltpu.make_async_remote_copy(
+                swap.at[0], swap.at[1], swap_sem.at[0], swap_sem.at[1],
+                device_id=(z * 2 + 1 - core, pool), device_id_type=MESH,
+            )
+            swap_copy.start()
         for i in batch:
             wait_bytes(r2.at[i], query_sem.at[i])
             for n in (i, 4 + i):
@@ -292,28 +295,36 @@
 
     s5[...] = attention
     for i, offset in enumerate(POOL_OFFSETS):
-        pool_send(s5, r5.at[pool], 5, offset)
-    r5[pool] = attention
+        pltpu.make_async_remote_copy(
+            s5, r5.at[i], send_sem.at[5], recv_sem.at[5 if i < FAR_ROWS else 8],
+            device_id=(head, pool_peer(offset)), device_id_type=MESH,
+        ).start()
     later[3].wait()
     last.wait()
-    wait_bytes(first15(r5), recv_sem.at[5])
-    x5[...] = r5[...].astype(F32).reshape(512, 128)
+
+    def place_rows(source, block):
+        x5[pl.ds(pl.multiple_of(source * 32, 32), 32), :] = block.astype(F32)
+
+    place_rows(pool, s5[...])
+    wait_bytes(r5.at[pl.ds(FAR_ROWS, 15 - FAR_ROWS)], recv_sem.at[8])
+    for i in range(FAR_ROWS, 15):
+        place_rows(pool_peer([4 - o for o in POOL_OFFSETS[i]]), r5[i])
+    wait_bytes(r5.at[pl.ds(0, FAR_ROWS)], recv_sem.at[5])
+    for i in range(FAR_ROWS):
+        place_rows(pool_peer([4 - o for o in POOL_OFFSETS[i]]), r5[i])
     rows = jnp.concatenate([x5[pl.ds(j, 64, stride=8), :].astype(BF16) for j in range(8)], axis=1)
 
     for c in range(4):
         part = jnp.dot(rows, wo[:, 256 * c : 256 * c + 256], preferred_element_type=F32)
         x6[:, 2 * c, :] = part[:, :128]
         x6[:, 2 * c + 1, :] = part[:, 128:]
-    for r in range(0, 64, 2):
-        pair = [x6[slot_smem[0, r + i]] for i in range(2)]
-        s6[r // 4, 8 * (r % 4) : 8 * (r % 4) + 16, :] = jnp.concatenate(pair, axis=0).astype(BF16)
-    for i, offset in enumerate(HEAD_OFFSETS):
-        head_send(s6.at[head_peer(offset)], r6.at[i], 6, recv_sem.at[6], offset)
-    wait_bytes(r6, recv_sem.at[6])
-    mixed = s6[head].astype(F32)
-    for i in range(15):
-        mixed = mixed + r6[i].astype(F32)
-    out_ref[...] = mixed
+    for i, offset in enumerate(OUTPUT_OFFSETS):
+        to = head_peer(offset)
+        row = [x6[slot_smem[0, to * 4 + k]] for k in range(4)]
+        s6[i, :16] = jnp.concatenate(row[:2], axis=0).astype(BF16)
+        s6[i, 16:] = jnp.concatenate(row[2:], axis=0).astype(BF16)
+        if i < 15:
+            head_send(s6.at[i], r6.at[i], 6, recv_sem.at[6 if i < FAR_OUTPUTS else 7], offset)
 
     wait_bytes(r1, send_sem.at[0])
     wait_bytes(rkv, send_sem.at[1])
@@ -326,7 +337,16 @@
         def _(buf=buf, phase=phase):
             wait_bytes(buf.at[0], send_sem.at[phase])
 
-    wait_bytes(first15(r5), send_sem.at[5])
+    wait_bytes(r5, send_sem.at[5])
+
+    mixed = s6[15].astype(F32)
+    wait_bytes(r6.at[pl.ds(FAR_OUTPUTS, 15 - FAR_OUTPUTS)], recv_sem.at[7])
+    for i in range(FAR_OUTPUTS, 15):
+        mixed = mixed + r6[i].astype(F32)
+    wait_bytes(r6.at[pl.ds(0, FAR_OUTPUTS)], recv_sem.at[6])
+    for i in range(FAR_OUTPUTS):
+        mixed = mixed + r6[i].astype(F32)
+    out_ref[...] = mixed
     wait_bytes(r6, send_sem.at[6])
 
 
@@ -360,14 +380,14 @@
             pltpu.VMEM((4, 2, 1, 128), F32),
             pltpu.VMEM((8, 1, 128), F32),
             pltpu.VMEM((32, 128), BF16),
-            pltpu.VMEM((16, 32, 128), BF16),
+            pltpu.VMEM((15, 32, 128), BF16),
             pltpu.VMEM((512, 128), F32),
             pltpu.VMEM((64, 8, 128), F32),
             pltpu.VMEM((16, 32, 128), BF16),
             pltpu.VMEM((15, 32, 128), BF16),
             pltpu.SemaphoreType.DMA((11,)),
             pltpu.SemaphoreType.DMA((7,)),
-            pltpu.SemaphoreType.DMA((7,)),
+            pltpu.SemaphoreType.DMA((9,)),
             pltpu.SemaphoreType.DMA((4,)),
             pltpu.SemaphoreType.DMA((2,)),
             pltpu.SemaphoreType.DMA((3, 8)),

time: 38.9 us -> 38.4 us (0.987)
  Pallas kernels: 38.2 us -> 37.7 us
    pallas_call x1, Pallas kernels: 38.2 us -> 37.7 us  [local(): pl.pallas_call(kernel, out_shape=pltpu.VMEM((32, 128), F32), in_specs=[hb...]
where the time goes in v5:
time: 38.4 us; the launch traced here: 38.3 us
  Pallas kernels  37.7 us (98%)
  local copies, waits for them, and re-layouts  0.62 us (2%)
    pallas_call x1, Pallas kernels, local(): pl.pallas_call(kernel, out_shape=pltpu.VMEM((32, 128), F32), in_specs=[hb...  37.7 us

profile of v5, /device:TPU:1, one launch (start us, length us, event | category | flops | bytes accessed | tf_op | source)
XLA Modules:
  0.0 38.3 jit_solution(3470394040993885755)
XLA Ops:
  0.0 37.7 %shard_map.91 = f32[32,128]{1,0:T(8,128)S(1)} custom-call(bf16[64,1024]{1,0:T(8,128)(2,1)} %hid_hbm.1, bf16[1024,1024]{1,0:T(8,128)(2,1)} %wq_hbm.1, bf16[64,1024]{1,0:T(8,128)(2,1)} %bitcast.4, bf16[64,1024]{1,0:T(8,128)(2,1)} %bitcast.5, bf16[1024,1024]{1,0:T(8,128)(2,1)} %wo_hbm.1, bf16[4,384,1024]{2,1,0:T(8,128)(2,1)} %k_hbm.1, ...), custom_call_target="tpu_custom_call" | custom-call | tf_op jit(solution)/shard_map/pallas_call | solution.py:356
  37.7 0.6 %reshape.11 = f32[4,1024]{1,0:T(4,128)} reshape(f32[32,128]{1,0:T(8,128)S(1)} %shard_map.91) | data formatting | bytes 32768 | tf_op jit(solution)/shard_map/reshape | solution.py:401

commit v6 on v5

--- a/solution.py
+++ b/solution.py
@@ -31,7 +31,7 @@
 ) + [(0, 0)]
 FAR_OUTPUTS = 6
 
-BATCHES = ((0,), (3,), (1,), (2,))
+BATCHES = ((0,), (3,), (2,), (1,))
 CHIP_OFFSETS = (3, 5, 4, 1, 7, 2, 6, 0)
 
 
@@ -285,7 +285,7 @@
     own_weight = jnp.exp(own - largest)
     denominator = jnp.sum(factor * pltpu.roll(parts, 96, 1), axis=0, keepdims=True) + own_weight
     shares = jnp.concatenate(
-        [factor / denominator, own_weight.astype(BF16).astype(F32) / denominator, jnp.zeros((119, 128), F32)], axis=0
+        [factor / denominator, own_weight.astype(BF16).astype(F32) / denominator, jnp.zeros((7, 128), F32)], axis=0
     ).T
     attention = shares[:32, 8:9] * spread(value_new)
     wait_bytes(r4, recv_sem.at[4])
@@ -314,10 +314,9 @@
         place_rows(pool_peer([4 - o for o in POOL_OFFSETS[i]]), r5[i])
     rows = jnp.concatenate([x5[pl.ds(j, 64, stride=8), :].astype(BF16) for j in range(8)], axis=1)
 
-    for c in range(4):
-        part = jnp.dot(rows, wo[:, 256 * c : 256 * c + 256], preferred_element_type=F32)
-        x6[:, 2 * c, :] = part[:, :128]
-        x6[:, 2 * c + 1, :] = part[:, 128:]
+    part = jnp.dot(rows, wo[...], preferred_element_type=F32)
+    for j in range(8):
+        x6[:, j, :] = part[:, 128 * j : 128 * j + 128]
     for i, offset in enumerate(OUTPUT_OFFSETS):
         to = head_peer(offset)
         row = [x6[slot_smem[0, to * 4 + k]] for k in range(4)]

time: 38.4 us -> 38.3 us (level)
  no operation moved by 1% of the time
where the time goes in v6:
time: 38.3 us; the launch traced here: 38.2 us
  Pallas kernels  37.6 us (98%)
  local copies, waits for them, and re-layouts  0.62 us (2%)
    pallas_call x1, Pallas kernels, local(): pl.pallas_call(kernel, out_shape=pltpu.VMEM((32, 128), F32), in_specs=[hb...  37.6 us

profile of v6, /device:TPU:1, one launch (start us, length us, event | category | flops | bytes accessed | tf_op | source)
XLA Modules:
  0.0 38.2 jit_solution(5101940950034184418)
XLA Ops:
  0.0 37.6 %shard_map.91 = f32[32,128]{1,0:T(8,128)S(1)} custom-call(bf16[64,1024]{1,0:T(8,128)(2,1)} %hid_hbm.1, bf16[1024,1024]{1,0:T(8,128)(2,1)} %wq_hbm.1, bf16[64,1024]{1,0:T(8,128)(2,1)} %bitcast.4, bf16[64,1024]{1,0:T(8,128)(2,1)} %bitcast.5, bf16[1024,1024]{1,0:T(8,128)(2,1)} %wo_hbm.1, bf16[4,384,1024]{2,1,0:T(8,128)(2,1)} %k_hbm.1, ...), custom_call_target="tpu_custom_call" | custom-call | tf_op jit(solution)/shard_map/pallas_call | solution.py:355
  37.6 0.6 %reshape.11 = f32[4,1024]{1,0:T(4,128)} reshape(f32[32,128]{1,0:T(8,128)S(1)} %shard_map.91) | data formatting | bytes 32768 | tf_op jit(solution)/shard_map/reshape | solution.py:400

commit v7 on v6

--- a/solution.py
+++ b/solution.py
@@ -32,7 +32,7 @@
 FAR_OUTPUTS = 6
 
 BATCHES = ((0,), (3,), (2,), (1,))
-CHIP_OFFSETS = (3, 5, 4, 1, 7, 2, 6, 0)
+CHIP_OFFSETS = (4, 1, 7, 2, 6, 3, 5, 0)
 
 
 def group_slot(dz):
@@ -207,12 +207,28 @@
         pairs = [(i, s) for i in batch for s in range(4)]
         arrived = {i: r2[i].astype(F32).reshape(2, 4, 8, 128) for i in batch}
         queries = [arrived[i][:, s].reshape(16, 128).astype(BF16) for i, s in pairs]
-        scores = [
-            jnp.concatenate(
-                [lax.dot_general(q, kc[i, c, s], ACROSS, preferred_element_type=F32) for c in range(2)], axis=1
+        scores = []
+        blank = jnp.zeros((16, 128), BF16)
+        for n in range(0, len(pairs), 2):
+            i, s = pairs[n]
+            both = jnp.concatenate(
+                [
+                    jnp.concatenate([queries[n], blank], axis=1),
+                    jnp.concatenate([blank, queries[n + 1]], axis=1),
+                ],
+                axis=0,
+            )
+            found = jnp.concatenate(
+                [
+                    lax.dot_general(
+                        both, jnp.concatenate([kc[i, c, s], kc[i, c, s + 1]], axis=1), ACROSS,
+                        preferred_element_type=F32,
+                    )
+                    for c in range(2)
+                ],
+                axis=1,
             ) * scale
-            for q, (i, s) in zip(queries, pairs)
-        ]
+            scores += [found[:16], found[16:]]
         tops = [
             jnp.max(jnp.where(valid[s], x, NEGATIVE), axis=1, keepdims=True)
             for x, (_, s) in zip(scores, pairs)

time: 38.3 us -> 38.2 us (level)
  no operation moved by 1% of the time
where the time goes in v7:
time: 38.2 us; the launch traced here: 38.1 us
  Pallas kernels  37.5 us (98%)
  local copies, waits for them, and re-layouts  0.62 us (2%)
    pallas_call x1, Pallas kernels, local(): pl.pallas_call(kernel, out_shape=pltpu.VMEM((32, 128), F32), in_specs=[hb...  37.5 us

profile of v7, /device:TPU:1, one launch (start us, length us, event | category | flops | bytes accessed | tf_op | source)
XLA Modules:
  0.0 38.1 jit_solution(591071314463328982)
XLA Ops:
  0.0 37.5 %shard_map.91 = f32[32,128]{1,0:T(8,128)S(1)} custom-call(bf16[64,1024]{1,0:T(8,128)(2,1)} %hid_hbm.1, bf16[1024,1024]{1,0:T(8,128)(2,1)} %wq_hbm.1, bf16[64,1024]{1,0:T(8,128)(2,1)} %bitcast.4, bf16[64,1024]{1,0:T(8,128)(2,1)} %bitcast.5, bf16[1024,1024]{1,0:T(8,128)(2,1)} %wo_hbm.1, bf16[4,384,1024]{2,1,0:T(8,128)(2,1)} %k_hbm.1, ...), custom_call_target="tpu_custom_call" | custom-call | tf_op jit(solution)/shard_map/pallas_call | solution.py:371
  37.5 0.6 %reshape.11 = f32[4,1024]{1,0:T(4,128)} reshape(f32[32,128]{1,0:T(8,128)S(1)} %shard_map.91) | data formatting | bytes 32768 | tf_op jit(solution)/shard_map/reshape | solution.py:416

commit v8 on v7

--- a/solution.py
+++ b/solution.py
@@ -239,8 +239,7 @@
         bottoms = [jnp.sum(x, axis=1, keepdims=True) for x in weights]
         weights = [x.astype(BF16) for x in weights]
         sums = [
-            jnp.dot(x[:, :384], vc[i, 0, s], preferred_element_type=F32)
-            + jnp.dot(x[:, 384:], vc[i, 1, s], preferred_element_type=F32)
+            jnp.dot(x, vc[i, :, s].reshape(768, 128), preferred_element_type=F32)
             for x, (i, s) in zip(weights, pairs)
         ]
         for n, i in enumerate(batch):

time: 38.2 us -> 38.2 us (level)
  no operation moved by 1% of the time
where the time goes in v8:
time: 38.2 us; the launch traced here: 38.1 us
  Pallas kernels  37.5 us (98%)
  local copies, waits for them, and re-layouts  0.62 us (2%)
    pallas_call x1, Pallas kernels, local(): pl.pallas_call(kernel, out_shape=pltpu.VMEM((32, 128), F32), in_specs=[hb...  37.5 us

profile of v8, /device:TPU:1, one launch (start us, length us, event | category | flops | bytes accessed | tf_op | source)
XLA Modules:
  0.0 38.1 jit_solution(4316413732446828737)
XLA Ops:
  0.0 37.5 %shard_map.91 = f32[32,128]{1,0:T(8,128)S(1)} custom-call(bf16[64,1024]{1,0:T(8,128)(2,1)} %hid_hbm.1, bf16[1024,1024]{1,0:T(8,128)(2,1)} %wq_hbm.1, bf16[64,1024]{1,0:T(8,128)(2,1)} %bitcast.4, bf16[64,1024]{1,0:T(8,128)(2,1)} %bitcast.5, bf16[1024,1024]{1,0:T(8,128)(2,1)} %wo_hbm.1, bf16[4,384,1024]{2,1,0:T(8,128)(2,1)} %k_hbm.1, ...), custom_call_target="tpu_custom_call" | custom-call | tf_op jit(solution)/shard_map/pallas_call | solution.py:370
  37.5 0.6 %reshape.11 = f32[4,1024]{1,0:T(4,128)} reshape(f32[32,128]{1,0:T(8,128)S(1)} %shard_map.91) | data formatting | bytes 32768 | tf_op jit(solution)/shard_map/reshape | solution.py:415
